TPU v7x, 32 devices: a whole 2x2x4 slice. The times are simulated.
32 devices in a mesh: req: 8 (over y, x, core), mlp: 4 (over z).
Axes of the slice: x: 2, y: 2, z: 4, core: 2. Of those that a mesh axis runs over, the one named last changes fastest.
Arguments:
- tokens: bfloat16 [1024, 2048], P(('req', 'mlp')), may hold values from -6 to 6
- cached_states: float32 [64, 8, 256, 512], P('req', 'mlp'), may hold values from -12 to 12
- prompt_lengths: int32 [64], P('req'), may hold values from 1 to 4096, as said below
- accepted: int32 [64], P('req'), may hold values from 1 to 16, as said below
- owner_slot: int32 [64], P('req'), may hold values from 0 to 63, as said below
- w_query: bfloat16 [2048, 2048], P(None, 'mlp'), may hold values from -0.125 to 0.125
- w_key: bfloat16 [2048, 2048], P(None, 'mlp'), may hold values from -0.125 to 0.125
- w_value: bfloat16 [2048, 4096], P(None, 'mlp'), may hold values from -0.125 to 0.125
- w_gate_ret: bfloat16 [2048, 4096], P(None, 'mlp'), may hold values from -0.125 to 0.125
- w_out: bfloat16 [4096, 2048], P('mlp'), may hold values from -0.09375 to 0.09375
- w_gate: bfloat16 [2048, 4096], P('req', 'mlp'), may hold values from -0.125 to 0.125
- w_up: bfloat16 [2048, 4096], P('req', 'mlp'), may hold values from -0.125 to 0.125
- w_down: bfloat16 [4096, 2048], P('mlp', 'req'), may hold values from -0.09375 to 0.09375
Outputs:
- mixed: bfloat16 [1024, 2048], P(('req', 'mlp'))
- new_states: float32 [64, 8, 256, 512], P('req', 'mlp')
Inputs may be any that keep to these rules, and one draw needn't show every extreme that they name: `prompt_lengths`: request r belongs to tenant k = (4 r) // 64, so the four tenants hold consecutive ranges of 16 requests; its prompt length is drawn evenly from 1 to 4^(k + 3). `accepted`: number of leading drafts of request r that are kept, drawn evenly for each request. A permutation of the requests; for request r on req block i = r // 8, owner_slot[r] = j * 8 + i + c with owner block j and 0 <= c < 1, and each pair (j, c) occurs exactly once within a block.
All inputs are finite; a program needn't handle non-finite values.
Results may differ from a plain program's by a relative error of at most 0.017.
Values may be sent and summed in bfloat16 or wider, within the bound.
A program may use at most 128 MiB of HBM per device.

v0:
```python
import math

import jax
import jax.numpy as jnp
from jax import lax
from jax.sharding import PartitionSpec as P

DRAFT = 16


epsilon = 1e-05


def layer_norm(inputs):
    average = jnp.mean(inputs, axis=-1, keepdims=True)
    centred = inputs - average
    variance = jnp.mean(centred * centred, axis=-1, keepdims=True)
    return centred * lax.rsqrt(variance + epsilon)


def decays(head_count, first_head):
    head_index = jnp.arange(head_count, dtype=jnp.float32) + first_head
    return 1.0 - jnp.exp2(-5.0 - head_index)


def rotate(inputs, positions):
    half_width = inputs.shape[-1] // 2
    frequencies = jnp.exp(
        -math.log(10000.0) * jnp.arange(half_width, dtype=jnp.float32) / half_width
    )
    angles = positions[:, :, None] * frequencies[None, None, :]
    cosine_part = jnp.cos(angles)[:, :, None, :]
    sine_part = jnp.sin(angles)[:, :, None, :]
    front_half = inputs[..., :half_width]
    back_half = inputs[..., half_width:]
    return jnp.concatenate(
        [
            front_half * cosine_part - back_half * sine_part,
            front_half * sine_part + back_half * cosine_part,
        ],
        axis=-1,
    )


def state_weights(states, accepted, gammas, draft_count):
    draft_pos = jnp.arange(draft_count, dtype=jnp.float32)
    accepted_f = accepted.astype(jnp.float32)
    exponent = accepted_f[:, None, None] - 1.0 - draft_pos[None, None, :]
    draft_weights = jnp.where(
        exponent >= 0, jnp.power(gammas[None, :, None], jnp.maximum(exponent, 0.0)), 0.0
    )
    old_part = jnp.power(gammas[None, :], accepted_f[:, None])[:, :, None, None] * states
    return (old_part, draft_weights)


def fold_update(key_rows, values, draft_weights):
    scaled = key_rows.astype(jnp.float32) * jnp.transpose(draft_weights, (0, 2, 1))[..., None]
    return jnp.einsum(
        "rshd,rshv->rhdv", scaled, values.astype(jnp.float32), precision=lax.Precision.HIGHEST
    )


def retain_outputs(queries, key_rows, values, states, gammas):
    draft_count = queries.shape[1]
    draft_pos = jnp.arange(draft_count, dtype=jnp.float32)
    distance = draft_pos[:, None] - draft_pos[None, :]
    decay_mask = jnp.where(
        distance[None] >= 0, jnp.power(gammas[:, None, None], jnp.maximum(distance, 0.0)[None]), 0.0
    )
    scores = jnp.einsum("rthd,rshd->rhts", queries, key_rows, preferred_element_type=jnp.float32)
    weights = (scores * decay_mask[None]).astype(jnp.bfloat16)
    within = jnp.einsum("rhts,rshv->rthv", weights, values, preferred_element_type=jnp.float32)
    carried = jnp.einsum(
        "rthd,rhdv->rthv", queries.astype(jnp.float32), states, precision=lax.Precision.HIGHEST
    )
    carried = carried * jnp.power(gammas[None, None, :, None], draft_pos[None, :, None, None] + 1.0)
    return within + carried


def per_device(
    tokens,
    cached_states,
    prompt_lengths,
    accepted,
    owner_slot,
    w_query,
    w_key,
    w_value,
    w_gate_ret,
    w_out,
    w_gate,
    w_up,
    w_down,
):
    requests = cached_states.shape[0]
    heads_here = cached_states.shape[1]
    key_width = cached_states.shape[2]
    value_width = cached_states.shape[3]
    draft_count = DRAFT
    per_peer = requests // lax.axis_size("req")
    first_head = (lax.axis_index("mlp") * heads_here).astype(jnp.float32)
    gammas = decays(heads_here, first_head)
    target_pos = owner_slot // requests * per_peer + owner_slot % per_peer
    local_ids = jnp.arange(requests, dtype=jnp.int32)
    send_order = jnp.sum(
        jnp.where(target_pos[None, :] == local_ids[:, None], local_ids[None, :], 0), axis=1
    )
    old_part, draft_weights = state_weights(cached_states, accepted, gammas, draft_count)
    group_rows = lax.all_gather(tokens, "mlp", axis=0, tiled=True)
    row_count = group_rows.shape[0]
    normed = layer_norm(group_rows.astype(jnp.float32)).astype(jnp.bfloat16)
    queries = jnp.dot(normed, w_query, preferred_element_type=jnp.float32).reshape(
        requests, draft_count, heads_here, key_width
    )
    key_rows = (
        jnp.dot(normed, w_key, preferred_element_type=jnp.float32) * (1.0 / math.sqrt(key_width))
    ).reshape(requests, draft_count, heads_here, key_width)
    values = (
        jnp.dot(normed, w_value, preferred_element_type=jnp.float32)
        .astype(jnp.bfloat16)
        .reshape(requests, draft_count, heads_here, value_width)
    )
    gate_ret = jnp.dot(normed, w_gate_ret, preferred_element_type=jnp.float32).reshape(
        requests, draft_count, heads_here, value_width
    )
    positions = (
        prompt_lengths[:, None] + jnp.arange(draft_count, dtype=jnp.int32)[None, :]
    ).astype(jnp.float32)
    rotated_q = rotate(queries, positions).astype(jnp.bfloat16)
    rotated_k = rotate(key_rows, positions).astype(jnp.bfloat16)
    fresh = old_part + fold_update(rotated_k, values, draft_weights)
    new_states = lax.all_to_all(
        jnp.take(fresh, send_order, axis=0).astype(jnp.bfloat16),
        "req",
        split_axis=0,
        concat_axis=0,
        tiled=True,
    ).astype(jnp.float32)
    outputs = retain_outputs(rotated_q, rotated_k, values, cached_states, gammas)
    joined = (
        (layer_norm(outputs) * jax.nn.silu(gate_ret))
        .astype(jnp.bfloat16)
        .reshape(row_count, heads_here * value_width)
    )
    partials = jnp.dot(joined, w_out, preferred_element_type=jnp.float32)
    share = tokens.shape[0]
    summed = lax.psum(partials.astype(jnp.bfloat16), "mlp").astype(jnp.float32)
    residual = group_rows.astype(jnp.float32) + summed
    hidden_in = layer_norm(residual).astype(jnp.bfloat16)
    residual_share = lax.dynamic_slice_in_dim(residual, lax.axis_index("mlp") * share, share, 0)
    gate_sum = jnp.dot(
        hidden_in,
        lax.all_gather(w_gate, "req", axis=0, tiled=True),
        preferred_element_type=jnp.float32,
    )
    up_sum = jnp.dot(
        hidden_in,
        lax.all_gather(w_up, "req", axis=0, tiled=True),
        preferred_element_type=jnp.float32,
    )
    hidden = (jax.nn.silu(gate_sum) * up_sum).astype(jnp.bfloat16)
    down_terms = jnp.dot(
        hidden,
        lax.all_gather(w_down, "req", axis=1, tiled=True),
        preferred_element_type=jnp.float32,
    )
    mixed = (
        residual_share
        + lax.psum_scatter(
            down_terms.astype(jnp.bfloat16), "mlp", scatter_dimension=0, tiled=True
        ).astype(jnp.float32)
    ).astype(jnp.bfloat16)
    return (mixed, new_states)


def solution(mesh):
    return jax.shard_map(
        per_device,
        mesh=mesh,
        in_specs=(
            P(("req", "mlp"), None),
            P("req", "mlp", None, None),
            P("req"),
            P("req"),
            P("req"),
            P(None, "mlp"),
            P(None, "mlp"),
            P(None, "mlp"),
            P(None, "mlp"),
            P("mlp", None),
            P("req", "mlp"),
            P("req", "mlp"),
            P("mlp", "req"),
        ),
        out_specs=(P(("req", "mlp"), None), P("req", "mlp", None, None)),
        check_vma=False,
    )
```

profile of v0, /device:TPU:0, one launch (start us, length us, event | category | flops | bytes accessed | tf_op | source)
XLA Modules:
  0.0 232.0 jit_solution(13857954737563837495)
XLA Ops:
  8.1 17.7 %all_gather.12 = bf16[128,2048]{1,0:T(8,128)(2,1)S(1)} all-gather(bf16[32,2048]{1,0:T(8,128)(2,1)} %param.13), channel_id=1, replica_groups=mesh['req'=8,'mlp'=4] {'mlp'}, dimensions={0}, use_global_device_ids=true | all-gather | bytes 655360 | tf_op jit(solution)/shard_map/all_gather | solution.py:109
  26.3 3.8 %fusion.32 = f32[128,1024]{1,0:T(8,128)} fusion(bf16[2048,1024]{1,0:T(8,128)(2,1)} %param.21, bf16[128,2048]{1,0:T(8,128)(2,1)S(1)} %all_gather.12, f32[128]{0:T(128)S(1)} %add_rsqrt_fusion.2, f32[128]{0:T(128)S(1)} %broadcast_multiply_fusion.2), kind=kOutput, calls=%fused_computation.85 | convolution fusion | flops 537919488 | bytes 5243904 | tf_op jit(solution)/shard_map/dot_general | solution.py:123
  30.0 1.5 reshape.275
  32.3 2.1 fusion.35
  34.6 2.9 %convolution_convert_fusion.2 = bf16[128,1024]{1,0:T(8,128)(2,1)S(1)} fusion(bf16[2048,1024]{1,0:T(8,128)(2,1)} %param.20, bf16[128,2048]{1,0:T(8,128)(2,1)S(1)} %all_gather.12, f32[128]{0:T(128)S(1)} %add_rsqrt_fusion.2, f32[128]{0:T(128)S(1)} %broadcast_multiply_fusion.2), kind=kOutput, calls=%fused_computation.16 | convolution fusion | flops 538050560 | bytes 4981760 | tf_op jit(solution)/shard_map/dot_general | solution.py:119
  38.6 6.2 %fusion.3 = f32[8,16,2,512]{3,1,2,0:T(8,128)S(1)} fusion(f32[8,2,256,512]{3,2,1,0:T(8,128)} %param.14, f32[16,2]{0,1:T(2,128)S(1)} %broadcast_power_fusion.1, bf16[8,16,2,128]{3,1,2,0:T(8,128)(2,1)S(1)} %get-tuple-element.12, bf16[8,16,2,128]{3,1,2,0:T(8,128)(2,1)S(1)} %get-tuple-element.13), kind=kOutput, calls=%fused_computation.14 | convolution fusion | flops 403046400 | bytes 9044096 | tf_op jit(solution)/shard_map/rthd,rhdv->rthv/dot_general | solution.py:73
  46.0 3.7 %convolution_convert_fusion.1 = bf16[128,2048]{1,0:T(8,128)(2,1)} fusion(bf16[128,1024]{1,0:T(8,128)(2,1)S(1)} %bitcast.25, bf16[1024,2048]{1,0:T(8,128)(2,1)} %param.22), kind=kOutput, calls=%fused_computation.4 | convolution fusion | flops 537133056 | bytes 4980736 | tf_op jit(solution)/shard_map/dot_general | solution.py:145
  49.8 0.5 all-gather.4.cloned.1.call-update
  50.4 0.5 all-gather.8.cloned.1.call-update
  52.0 8.5 %multiply_add_fusion = bf16[8,2,256,512]{3,2,1,0:T(8,128)(2,1)} fusion(f32[8,2,256,512]{3,2,1,0:T(8,128)} %param.14, f32[8,2]{1,0:T(8,128)S(1)} %broadcast_power_fusion, bf16[8,16,2,512]{3,2,1,0:T(2,128)(2,1)S(1)} %reshape.272, f32[8,16,2]{1,2,0:T(2,128)S(1)} %power_select_fusion.1, bf16[8,16,2,128]{3,1,2,0:T(8,128)(2,1)S(1)} %get-tuple-element.5, ...), kind=kOutput, calls=%fused_computation.2 | convolution fusion | flops 409272320 | bytes 12977216 | tf_op jit(solution)/shard_map/rshd,rshv->rhdv/dot_general | solution.py:58
  60.6 5.3 %gather_fusion = bf16[8,2,256,512]{3,2,1,0:T(8,128)(2,1)} fusion(bf16[8,2,256,512]{3,2,1,0:T(8,128)(2,1)} %multiply_add_fusion, s32[1024]{0:T(1024)S(1)} %pad_clamp_fusion), kind=kCustom, calls=%fused_computation | custom fusion | bytes 8388640 | tf_op jit(solution)/shard_map/jit(_take)/gather | solution.py:133
  65.9 5.5 %select_convert_fusion = bf16[8,2,256,512]{3,2,1,0:T(8,128)(2,1)} fusion(bf16[8,2,256,512]{3,2,1,0:T(8,128)(2,1)} %gather_fusion, pred[8]{0:T(512)(128)(4,1)S(1)} %compare_and_fusion), kind=kLoop, calls=%fused_computation.1 | loop fusion | flops 2097152 | bytes 8388616 | tf_op jit(solution)/shard_map/convert_element_type | solution.py:133
  71.4 4.6 %all-to-all-start = ((bf16[8,2,256,512]{3,2,1,0:T(8,128)(2,1)}), bf16[8,2,256,512]{3,2,1,0:T(8,128)(2,1)}, u32[]{:S(2)}, u32[]{:S(2)}) async-start(bf16[8,2,256,512]{3,2,1,0:T(8,128)(2,1)} %select_convert_fusion), calls=%async_computation.1 | async-start | bytes 8388608 | tf_op jit(solution)/shard_map/all_to_all | solution.py:132
  76.0 13.9 %all-reduce.2.cloned.1.call-done = bf16[128,2048]{1,0:T(8,128)(2,1)} async-done(((bf16[128,2048]{1,0:T(8,128)(2,1)}), bf16[128,2048]{1,0:T(8,128)(2,1)}) %all-reduce.2.cloned.1.call-update) | async-done | bytes 524304 | tf_op jit(solution)/shard_map/psum | solution.py:147
  89.9 2.2 convert_add_fusion
  92.2 1.3 multiply_reduce_fusion
  93.5 6.8 %all-gather.4.cloned.1.call-done = bf16[2048,1024]{1,0:T(8,128)(2,1)} async-done(((bf16[256,1024]{1,0:T(8,128)(2,1)}), bf16[2048,1024]{1,0:T(8,128)(2,1)}) %all-gather.4.cloned.1.call-update) | async-done | bytes 4194320 | tf_op jit(solution)/shard_map/all_gather | solution.py:153
  100.3 3.3 %fusion.31 = f32[128,1024]{1,0:T(8,128)S(1)} fusion(bf16[2048,1024]{1,0:T(8,128)(2,1)} %all-gather.4.cloned.1.call-done, f32[128]{0:T(128)S(1)} %add_rsqrt_fusion.1, f32[128]{0:T(128)S(1)} %broadcast_multiply_fusion.1, bf16[128,2048]{1,0:T(8,128)(2,1)} %all-reduce.2.cloned.1.call-done, bf16[128,2048]{1,0:T(8,128)(2,1)S(1)} %all_gather.12), kind=kOutput, calls=%fused_computation.84 | convolution fusion | flops 538443776 | bytes 5768192 | tf_op jit(solution)/shard_map/dot_general | solution.py:151
  103.6 53.2 %all-gather.8.cloned.1.call-done = bf16[1024,2048]{1,0:T(8,128)(2,1)} async-done(((bf16[1024,256]{1,0:T(8,128)(2,1)}), bf16[1024,2048]{1,0:T(8,128)(2,1)}) %all-gather.8.cloned.1.call-update) | async-done | bytes 4194320 | tf_op jit(solution)/shard_map/all_gather | solution.py:164
  156.8 38.3 %all-gather.6.cloned.1.call-done = bf16[2048,1024]{1,0:T(8,128)(2,1)} async-done(((bf16[256,1024]{1,0:T(8,128)(2,1)}), bf16[2048,1024]{1,0:T(8,128)(2,1)}) %all-gather.6.cloned.1.call-update) | async-done | bytes 4194320 | tf_op jit(solution)/shard_map/all_gather | solution.py:158
  195.1 5.8 %convolution_convert_fusion = bf16[128,2048]{1,0:T(8,128)(2,1)} fusion(bf16[1024,2048]{1,0:T(8,128)(2,1)} %all-gather.8.cloned.1.call-done, bf16[2048,1024]{1,0:T(8,128)(2,1)} %all-gather.6.cloned.1.call-done, f32[128,1024]{1,0:T(8,128)S(1)} %fusion.31, f32[128]{0:T(128)S(1)} %add_rsqrt_fusion.1, f32[128]{0:T(128)S(1)} %broadcast_multiply_fusion.1, ...), kind=kOutput, calls=%fused_computation.3 | convolution fusion | flops 1076363264 | bytes 10486784 | tf_op jit(solution)/shard_map/dot_general | solution.py:162
  201.0 6.9 %convert_element_type.80 = f32[8,2,256,512]{3,2,1,0:T(8,128)} convert(bf16[8,2,256,512]{3,2,1,0:T(8,128)(2,1)} %all-to-all-done) | non-fusion elementwise | flops 2097152 | bytes 12582912 | tf_op jit(solution)/shard_map/convert_element_type | solution.py:138
  207.8 14.9 %reduce-scatter.2.cloned.1.call-done = bf16[32,2048]{1,0:T(8,128)(2,1)} async-done(((bf16[128,2048]{1,0:T(8,128)(2,1)}), bf16[32,2048]{1,0:T(8,128)(2,1)}) %reduce-scatter.2.cloned.1.call-update) | async-done | bytes 131088 | tf_op jit(solution)/shard_map/reduce_scatter | solution.py:169
  222.7 1.7 add_convert_fusion
  (60 shorter events, 4.9 us)
Async XLA Ops:
  8.0 23.6 %copy-start = (bf16[2048,512]{1,0:T(8,128)(2,1)S(1)}, bf16[2048,512]{1,0:T(8,128)(2,1)}, u32[]{:S(2)}) copy-start(bf16[2048,512]{1,0:T(8,128)(2,1)} %param.19) | copy-start | bytes 6291460
  8.0 81.9 %all-reduce.2.cloned.1.call-start = ((), (), s32[]{:S(2)}) async-start(), calls=%async_computation.2 | async-start | bytes 1048576 | tf_op jit(solution)/shard_map/psum | solution.py:147
  30.0 4.5 %copy-start.3 = (s32[8]{0:T(128)S(1)}, s32[8]{0:T(128)}, u32[]{:S(2)}) copy-start(s32[8]{0:T(128)} %param.15) | copy-start | bytes 100
  45.7 5.8 %copy-start.5 = (s32[8]{0:T(128)S(1)}, s32[8]{0:T(128)}, u32[]{:S(2)}) copy-start(s32[8]{0:T(128)} %param.16) | copy-start | bytes 100
  45.7 5.8 %copy-start.4 = (s32[8]{0:T(128)S(1)}, s32[8]{0:T(128)}, u32[]{:S(2)}) copy-start(s32[8]{0:T(128)} %param.17) | copy-start | bytes 100
  49.7 50.6 %all-gather.4.cloned.1.call-start = ((), (), s32[]{:S(2)}) async-start(), calls=%async_computation.3 | async-start | bytes 4718592 | tf_op jit(solution)/shard_map/all_gather | solution.py:153
  50.3 106.5 %all-gather.8.cloned.1.call-start = ((), (), s32[]{:S(2)}) async-start(), calls=%async_computation.5 | async-start | bytes 4718592 | tf_op jit(solution)/shard_map/all_gather | solution.py:164
  50.9 144.2 %all-gather.6.cloned.1.call-start = ((), (), s32[]{:S(2)}) async-start(), calls=%async_computation.4 | async-start | bytes 4718592 | tf_op jit(solution)/shard_map/all_gather | solution.py:158
  71.4 129.6 %all-to-all-start = ((bf16[8,2,256,512]{3,2,1,0:T(8,128)(2,1)}), bf16[8,2,256,512]{3,2,1,0:T(8,128)(2,1)}, u32[]{:S(2)}, u32[]{:S(2)}) async-start(bf16[8,2,256,512]{3,2,1,0:T(8,128)(2,1)} %select_convert_fusion), calls=%async_computation.1 | async-start | bytes 8388608 | tf_op jit(solution)/shard_map/all_to_all | solution.py:132
  76.0 146.7 %reduce-scatter.2.cloned.1.call-start = ((), (), s32[]{:S(2)}) async-start(), calls=%async_computation.6 | async-start | bytes 655360 | tf_op jit(solution)/shard_map/reduce_scatter | solution.py:169
  89.9 105.2 %copy-start.2 = (bf16[128,2048]{1,0:T(8,128)(2,1)S(1)}, bf16[128,2048]{1,0:T(8,128)(2,1)}, u32[]{:S(2)}) copy-start(bf16[128,2048]{1,0:T(8,128)(2,1)} %all-reduce.2.cloned.1.call-done) | copy-start | bytes 1572868
  200.9 23.5 %copy-start.1 = (bf16[2048,512]{1,0:T(8,128)(2,1)S(1)}, bf16[2048,512]{1,0:T(8,128)(2,1)}, u32[]{:S(2)}) copy-start(bf16[2048,512]{1,0:T(8,128)(2,1)} %param.19) | copy-start | bytes 6291460
Sparse Core Ops, SparseCore 0:
  49.8 40.0 all-reduce.1
  201.1 21.6 reduce-scatter.1
Sparse Core Ops, SparseCore 1:
  52.1 48.1 all-gather.3
  102.0 54.7 all-gather.7
  158.6 36.5 all-gather.5
where the time goes:
time: 233 us; the launch traced here: 232 us
  waiting for transfers between devices  129 us (55%)
  matrix products  37.1 us (16%)
  other arithmetic  19.6 us (8%)
  blocking collectives  17.7 us (8%)
  between operations  16 us (7%)
  local copies, waits for them, and re-layouts  8.08 us (3%)
  starting transfers between devices  4.99 us (2%)
    all_gather x1, waiting for transfers between devices, per_device(): lax.all_gather(w_down, 'req', axis=1, tiled=True)  53.2 us
    all_gather x1, waiting for transfers between devices, per_device(): lax.all_gather(w_up, 'req', axis=0, tiled=True)  38.3 us
    all_gather x1, blocking collectives, per_device(): group_rows = lax.all_gather(tokens, 'mlp', axis=0, tiled=True)  17.7 us
    reduce_scatter x1, waiting for transfers between devices, per_device(): lax.psum_scatter(down_terms.astype(jnp.bfloat16), 'mlp', scatter_dimensio...  14.9 us
    psum x1, waiting for transfers between devices, per_device(): summed = lax.psum(partials.astype(jnp.bfloat16), 'mlp').astype(jnp.float32)  13.9 us
    dot_general x1, matrix products, fold_update(): jnp.einsum('rshd,rshv->rhdv', scaled, values.astype(jnp.float32), precisi...  8.54 us
    convert_element_type x1, other arithmetic, per_device(): new_states = lax.all_to_all(jnp.take(fresh, send_order, axis=0).astype(jn...  6.88 us
    all_gather x1, waiting for transfers between devices, per_device(): lax.all_gather(w_gate, 'req', axis=0, tiled=True)  6.78 us
  transfers between devices with their start and end apart: 6, of which 5 were waited for; matrix products, arithmetic and copies ran while one was open for 17% of the time, Pallas kernels for 0%

commit v1 on v0

v1 whole, which is shorter than its diff:
```python
import functools
import math

import jax
import jax.numpy as jnp
from jax import lax
from jax.experimental import pallas as pl
from jax.experimental.pallas import tpu as pltpu
from jax.sharding import PartitionSpec as P

DRAFT = 16


epsilon = 1e-05


def layer_norm(inputs):
    average = jnp.mean(inputs, axis=-1, keepdims=True)
    centred = inputs - average
    variance = jnp.mean(centred * centred, axis=-1, keepdims=True)
    return centred * lax.rsqrt(variance + epsilon)


def decays(head_count, first_head):
    head_index = jnp.arange(head_count, dtype=jnp.float32) + first_head
    return 1.0 - jnp.exp2(-5.0 - head_index)


MESH = pl.DeviceIdType.MESH
F32 = jnp.float32
BF16 = jnp.bfloat16


def mm(a, b):
    return jnp.dot(a, b, preferred_element_type=F32)


def kernel(
    n,
    m,
    order,
    old_scale,
    cosine,
    sine,
    mask,
    carry,
    fold,
    tokens,
    states,
    w_query,
    w_key,
    w_value,
    w_gate_ret,
    w_out,
    w_gate,
    w_up,
    w_down,
    mixed,
    moved,
    wq,
    wk,
    wv,
    wgr,
    wo,
    st,
    fg,
    fu,
    fd,
    tok,
    normed,
    rq,
    ksc,
    vals,
    rk_h,
    gated,
    outs,
    joined,
    part,
    part_in,
    res,
    hid,
    hs,
    part2,
    part2_in,
    send_buf,
    load_sem,
    tok_s,
    tok_r,
    part_s,
    part_r,
    hid_s,
    hid_r,
    part2_s,
    part2_r,
    w_s,
    w_r,
    st_s,
    st_r,
):
    me = lax.axis_index("req")
    mj = lax.axis_index("mlp")
    share, width = tokens.shape
    requests, heads, dk, dv = states.shape
    rows = m * share
    half = dk // 2
    per_peer = requests // n
    draft = DRAFT

    barrier = pltpu.get_barrier_semaphore()
    for k in range(1, n):
        pl.semaphore_signal(
            barrier, inc=1, device_id={"req": lax.rem(me + k, n)}, device_id_type=MESH
        )
    for k in range(1, m):
        pl.semaphore_signal(
            barrier, inc=1, device_id={"mlp": lax.rem(mj + k, m)}, device_id_type=MESH
        )

    loads = []
    for a, b in (
        (tokens, tok.at[mj]),
        (w_query, wq),
        (w_key, wk),
        (w_value, wv),
        (w_gate_ret, wgr),
        (states, st),
        (w_out, wo),
        (w_gate, fg.at[me]),
        (w_up, fu.at[me]),
        (w_down, fd.at[me]),
    ):
        copy = pltpu.make_async_copy(a, b, load_sem.at[len(loads)])
        copy.start()
        loads.append(copy)

    pl.semaphore_wait(barrier, n + m - 2)

    def mlp_copies(pick, dst, s, r):
        copies = []
        for k in range(1, m):
            peer = lax.rem(mj + k, m)
            copies.append(
                pltpu.make_async_remote_copy(
                    src_ref=pick(peer),
                    dst_ref=dst(k),
                    send_sem=s.at[k - 1],
                    recv_sem=r.at[k - 1],
                    device_id={"mlp": peer},
                    device_id_type=MESH,
                )
            )
        for copy in copies:
            copy.start()
        return copies

    tok_copies = mlp_copies(lambda peer: tokens, lambda k: tok.at[mj], tok_s, tok_r)

    cut = w_down.shape[0] // 2
    first = pl.ds(0, cut)
    second = pl.ds(cut, cut)

    def pieces(owner, own):
        if own:
            source = (w_gate, w_down.at[first], w_up, w_down.at[second])
        else:
            source = None
        there = (fg.at[owner], fd.at[owner, first], fu.at[owner], fd.at[owner, second])
        return source or there, there

    w_copies = {}

    def send_shard(owner, own, peer, slot, which=(0, 1, 2, 3)):
        source, there = pieces(owner, own)
        for i in which:
            copy = pltpu.make_async_remote_copy(
                src_ref=source[i],
                dst_ref=there[i],
                send_sem=w_s.at[slot, i],
                recv_sem=w_r.at[slot, i],
                device_id={"req": peer},
                device_id_type=MESH,
            )
            copy.start()
            w_copies[slot, i] = copy

    def arrived(slot, which=(0, 1, 2, 3)):
        for i in which:
            w_copies[slot, i].wait_recv()

    def flip(bits):
        out = me
        for bit in (1, 2, 4):
            if bits & bit:
                out = out + bit - 2 * bit * lax.rem(out // bit, 2)
        return out

    if n == 8:
        send_shard(me, True, flip(2), 0)
        send_shard(me, True, flip(4), 1)
        send_shard(me, True, flip(1), 2)
    else:
        for k in range(1, n):
            send_shard(me, True, lax.rem(me + k, n), k - 1)

    loads[0].wait()
    for copy in tok_copies:
        copy.wait_recv()
    normed[...] = layer_norm(tok[...].astype(F32).reshape(rows, width)).astype(BF16)
    cos_part, sin_part = cosine[...], sine[...]

    def turned(v):
        front, back = v[:, :half], v[:, half:]
        return jnp.concatenate(
            [front * cos_part - back * sin_part, front * sin_part + back * cos_part], axis=-1
        ).astype(BF16)

    loads[1].wait()
    loads[2].wait()
    for h in range(heads):
        cols = pl.ds(h * dk, dk)
        rq[:, cols] = turned(mm(normed[...], wq[:, cols]))
        rk = turned(mm(normed[...], wk[:, cols]) * (1.0 / math.sqrt(dk)))
        rk_h[:, cols] = rk
        ksc[:, :, cols] = (
            (rk.astype(F32) * fold[h]).astype(BF16).reshape(requests, draft, dk)
        )
    loads[3].wait()
    loads[4].wait()
    for h in range(heads):
        cols = pl.ds(h * dv, dv)
        vals[:, :, cols] = mm(normed[...], wv[:, cols]).astype(BF16).reshape(
            requests, draft, dv
        )
        g = mm(normed[...], wgr[:, cols])
        gated[:, cols] = g / (1.0 + jnp.exp(-g))
    loads[5].wait()

    @pl.loop(0, requests)
    def _(r):
        here = pl.ds(pl.multiple_of(r * draft, draft), draft)
        for h in range(heads):
            outs[here, h * dv : (h + 1) * dv] = mm(
                rq[here, h * dk : (h + 1) * dk], st[r, h].astype(BF16)
            )

    for h in range(heads):
        cols = pl.ds(h * dk, dk)
        vcols = pl.ds(h * dv, dv)
        scores = lax.dot_general(
            rq[:, cols], rk_h[:, cols], (((1,), (1,)), ((), ())), preferred_element_type=F32
        )
        weights = (scores * mask[h]).astype(BF16)
        out = mm(weights, vals[:, :, vcols].reshape(rows, dv)) + outs[:, vcols] * carry[h]
        joined[:, vcols] = (layer_norm(out) * gated[:, vcols]).astype(BF16)

    loads[6].wait()
    step = min(512, width)

    @pl.loop(0, width // step)
    def _(c):
        cols = pl.ds(pl.multiple_of(c * step, step), step)
        part[:, :, cols] = mm(joined[...], wo[:, cols]).astype(BF16).reshape(m, share, step)

    part_copies = mlp_copies(
        lambda peer: part.at[peer], lambda k: part_in.at[k - 1], part_s, part_r
    )

    if n == 8:
        arrived(0)
        send_shard(flip(2), False, flip(4), 3, (0, 1))
        arrived(1)
        send_shard(flip(4), False, flip(2), 3, (2, 3))
        send_shard(flip(2), False, flip(1), 4)
        send_shard(flip(4), False, flip(1), 5)

    st_copies = []

    def fresh(p):
        r = order[p]
        for h in range(heads):
            update = lax.dot_general(
                ksc[r, :, h * dk : (h + 1) * dk],
                vals[r, :, h * dv : (h + 1) * dv],
                (((0,), (0,)), ((), ())),
                preferred_element_type=F32,
            )
            send_buf[p, h] = (old_scale[r, h] * st[r, h] + update).astype(BF16)

    pl.loop(0, requests)(fresh)
    mine = pl.ds(me * per_peer, per_peer)
    for k in range(1, n):
        peer = lax.rem(me + k, n)
        copy = pltpu.make_async_remote_copy(
            src_ref=send_buf.at[pl.ds(peer * per_peer, per_peer)],
            dst_ref=moved.at[mine],
            send_sem=st_s.at[k - 1],
            recv_sem=st_r.at[k - 1],
            device_id={"req": peer},
            device_id_type=MESH,
        )
        copy.start()
        st_copies.append(copy)
    keep = pltpu.make_async_copy(send_buf.at[mine], moved.at[mine], load_sem.at[10])
    keep.start()

    total = part[mj].astype(F32)
    for k, copy in enumerate(part_copies):
        copy.wait_recv()
        total = total + part_in[k].astype(F32)
    residual = tok[mj].astype(F32) + total
    res[...] = residual
    hid[mj] = layer_norm(residual).astype(BF16)
    hid_copies = mlp_copies(lambda peer: hid.at[mj], lambda k: hid.at[mj], hid_s, hid_r)

    if n == 8:
        arrived(3)
        send_shard(flip(6), False, flip(1), 6)
        last = (2, 4, 5, 6)
    else:
        last = tuple(range(n - 1))
    for copy in hid_copies:
        copy.wait_recv()
    for slot in last:
        arrived(slot)
    for copy in loads[7:]:
        copy.wait()

    rows_in = fg.shape[1]
    inner = fg.shape[2]
    tile = min(256, inner)

    @pl.loop(0, inner // tile)
    def _(c):
        cols = pl.ds(pl.multiple_of(c * tile, tile), tile)
        g = jnp.zeros((rows, tile), F32)
        u = jnp.zeros((rows, tile), F32)
        for i in range(n):
            a = hid[:, :, i * rows_in : (i + 1) * rows_in].reshape(rows, rows_in)
            g = g + mm(a, fg[i, :, cols])
            u = u + mm(a, fu[i, :, cols])
        hs[:, cols] = (g / (1.0 + jnp.exp(-g)) * u).astype(BF16)

    wide = fd.shape[2]

    @pl.loop(0, n)
    def _(i):
        cols = pl.ds(pl.multiple_of(i * wide, wide), wide)
        part2[:, :, cols] = mm(hs[...], fd[i]).astype(BF16).reshape(m, share, wide)

    part2_copies = mlp_copies(
        lambda peer: part2.at[peer], lambda k: part2_in.at[k - 1], part2_s, part2_r
    )
    total = part2[mj].astype(F32)
    for k, copy in enumerate(part2_copies):
        copy.wait_recv()
        total = total + part2_in[k].astype(F32)
    mixed[...] = (res[...] + total).astype(BF16)

    keep.wait()
    for copy in st_copies:
        copy.wait()
    for copy in tok_copies + part_copies + hid_copies + part2_copies:
        copy.wait_send()
    for copy in w_copies.values():
        copy.wait_send()


def per_device(
    tokens,
    cached_states,
    prompt_lengths,
    accepted,
    owner_slot,
    w_query,
    w_key,
    w_value,
    w_gate_ret,
    w_out,
    w_gate,
    w_up,
    w_down,
):
    requests, heads, dk, dv = cached_states.shape
    n = lax.axis_size("req")
    m = lax.axis_size("mlp")
    share, width = tokens.shape
    rows = requests * DRAFT
    per_peer = requests // n
    gammas = decays(heads, (lax.axis_index("mlp") * heads).astype(F32))
    target_pos = owner_slot // requests * per_peer + owner_slot % per_peer
    ids = jnp.arange(requests, dtype=jnp.int32)
    order = jnp.sum(jnp.where(target_pos[None, :] == ids[:, None], ids[None, :], 0), axis=1)
    kept = accepted.astype(F32)
    old_scale = jnp.power(gammas[None, :], kept[:, None])
    draft_pos = jnp.arange(DRAFT, dtype=F32)
    exponent = kept[:, None] - 1.0 - draft_pos[None, :]
    fold = jnp.where(
        exponent[None] >= 0,
        jnp.power(gammas[:, None, None], jnp.maximum(exponent, 0.0)[None]),
        0.0,
    ).reshape(heads, rows, 1)
    row = jnp.arange(rows, dtype=jnp.int32)
    distance = (row[:, None] - row[None, :]).astype(F32)
    same = (row[:, None] // DRAFT == row[None, :] // DRAFT) & (distance >= 0)
    mask = jnp.where(
        same[None], jnp.power(gammas[:, None, None], jnp.maximum(distance, 0.0)[None]), 0.0
    )
    carry = jnp.power(
        gammas[:, None, None], ((row % DRAFT).astype(F32) + 1.0)[None, :, None]
    )
    half = dk // 2
    frequencies = jnp.exp(-math.log(10000.0) * jnp.arange(half, dtype=F32) / half)
    positions = (
        (prompt_lengths[:, None] + jnp.arange(DRAFT, dtype=jnp.int32)[None, :])
        .astype(F32)
        .reshape(rows, 1)
    )
    angles = positions * frequencies[None, :]
    vmem = pl.BlockSpec(memory_space=pltpu.VMEM)
    smem = pl.BlockSpec(memory_space=pltpu.SMEM)
    hbm = pl.BlockSpec(memory_space=pl.ANY)
    dma = pltpu.SemaphoreType.DMA

    def v(shape, dtype=BF16):
        return pltpu.VMEM(shape, dtype)

    mixed, moved = pl.pallas_call(
        functools.partial(kernel, n, m),
        out_shape=(
            jax.ShapeDtypeStruct((share, width), BF16),
            jax.ShapeDtypeStruct((requests, heads, dk, dv), BF16),
        ),
        in_specs=[smem] * 2 + [vmem] * 5 + [hbm] * 10,
        out_specs=(vmem, hbm),
        scratch_shapes=[
            v(w_query.shape),
            v(w_key.shape),
            v(w_value.shape),
            v(w_gate_ret.shape),
            v(w_out.shape),
            v(cached_states.shape, F32),
            v((n,) + w_gate.shape),
            v((n,) + w_up.shape),
            v((n,) + w_down.shape),
            v((m, share, width)),
            v((rows, width)),
            v((rows, heads * dk)),
            v((requests, DRAFT, heads * dk)),
            v((requests, DRAFT, heads * dv)),
            v((rows, heads * dk)),
            v((rows, heads * dv), F32),
            v((rows, heads * dv), F32),
            v((rows, heads * dv)),
            v((m, share, width)),
            v((m - 1, share, width)),
            v((share, width), F32),
            v((m, share, width)),
            v((rows, w_gate.shape[1])),
            v((m, share, width)),
            v((m - 1, share, width)),
            v(cached_states.shape),
            dma((11,)),
            dma((m - 1,)),
            dma((m - 1,)),
            dma((m - 1,)),
            dma((m - 1,)),
            dma((m - 1,)),
            dma((m - 1,)),
            dma((m - 1,)),
            dma((m - 1,)),
            dma((n - 1, 4)),
            dma((n - 1, 4)),
            dma((n - 1,)),
            dma((n - 1,)),
        ],
        compiler_params=pltpu.CompilerParams(
            collective_id=0, has_side_effects=True, vmem_limit_bytes=60 * 1024 * 1024
        ),
    )(
        order,
        old_scale,
        jnp.cos(angles),
        jnp.sin(angles),
        mask,
        carry,
        fold,
        tokens,
        cached_states,
        w_query,
        w_key,
        w_value,
        w_gate_ret,
        w_out,
        w_gate,
        w_up,
        w_down,
    )
    return (mixed, moved.astype(F32))


def solution(mesh):
    return jax.shard_map(
        per_device,
        mesh=mesh,
        in_specs=(
            P(("req", "mlp"), None),
            P("req", "mlp", None, None),
            P("req"),
            P("req"),
            P("req"),
            P(None, "mlp"),
            P(None, "mlp"),
            P(None, "mlp"),
            P(None, "mlp"),
            P("mlp", None),
            P("req", "mlp"),
            P("req", "mlp"),
            P("mlp", "req"),
        ),
        out_specs=(P(("req", "mlp"), None), P("req", "mlp", None, None)),
        check_vma=False,
    )
```

time: 233 us -> 122 us (0.52)
  waiting for transfers between devices: 129 us -> 0 us
  Pallas kernels: 0 us -> 105 us
  matrix products: 37.1 us -> 0 us
  blocking collectives: 17.7 us -> 0 us
  between operations: 16 us -> 0.68 us
  local copies, waits for them, and re-layouts: 8.08 us -> 1.65 us
  other arithmetic: 19.6 us -> 13.2 us
  starting transfers between devices: 4.99 us -> 0 us
    pallas_call x0 -> x1, Pallas kernels: none -> 105 us  [per_device(): pl.pallas_call(functools.partial(kernel, n, m), out_shape=(jax.ShapeDtype...]
    all_gather x3 -> x0, waiting for transfers between devices: 98.3 us -> none  [the longest x1 53.2 us: per_device(): lax.all_gather(w_down, 'req', axis=1, tiled=True)]
    dot_general x10 -> x0, matrix products: 37.1 us -> none  [the longest x1 8.54 us: fold_update(): jnp.einsum('rshd,rshv->rhdv', scaled, values.astype(jnp.float32), precisi...]
    all_gather x1 -> x0, blocking collectives: 17.7 us -> none  [per_device(): group_rows = lax.all_gather(tokens, 'mlp', axis=0, tiled=True)]
    reduce_scatter x1 -> x0, waiting for transfers between devices: 14.9 us -> none  [per_device(): lax.psum_scatter(down_terms.astype(jnp.bfloat16), 'mlp', scatter_dimensio...]
    psum x1 -> x0, waiting for transfers between devices: 13.9 us -> none  [per_device(): summed = lax.psum(partials.astype(jnp.bfloat16), 'mlp').astype(jnp.float32)]
    convert_element_type x6 -> x3, other arithmetic: 14.4 us -> 8.16 us  [the longest x1 6.77 us: per_device(): return (mixed, moved.astype(F32))]
    gather x1 -> x0, local copies, waits for them, and re-layouts: 5.28 us -> none  [per_device(): jnp.take(fresh, send_order, axis=0).astype(jnp.bfloat16)]
  transfers between devices with their start and end apart: 6 -> 0, of which waited for: 5 -> 0; matrix products, arithmetic and copies ran while one was open for 17% -> 0% of each run, Pallas kernels for 0% -> 0%
where the time goes in v1:
time: 122 us; the launch traced here: 120 us
  Pallas kernels  105 us (86%)
  other arithmetic  13.2 us (11%)
  local copies, waits for them, and re-layouts  1.65 us (1%)
    pallas_call x1, Pallas kernels, per_device(): pl.pallas_call(functools.partial(kernel, n, m), out_shape=(jax.ShapeDtype...  105 us
    convert_element_type x1, other arithmetic, per_device(): return (mixed, moved.astype(F32))  6.77 us

profile of v1, /device:TPU:0, one launch (start us, length us, event | category | flops | bytes accessed | tf_op | source)
XLA Modules:
  0.0 120.4 jit_solution(10017634915367100328)
XLA Ops:
  0.6 0.7 and_select_fusion.2
  1.3 0.7 select_reduce_fusion.order
  2.0 0.7 broadcast_add_fusion
  2.7 0.7 convert_element_type.39
  3.3 0.7 broadcast_power_fusion.1.old_scale
  4.0 0.1 sub.93
  4.1 0.1 sub.94
  4.2 0.7 add_convert_fusion
  4.9 0.1 convert_element_type.41
  5.0 0.1 sub.96
  5.1 0.1 fusion
  5.2 0.9 power_select_fusion.1.mask
  6.1 1.0 multiply_sine_fusion
  7.1 1.0 power_select_fusion
  8.1 104.9 %shard_map.140 = (bf16[32,2048]{1,0:T(8,128)(2,1)}, bf16[8,2,256,512]{3,2,1,0:T(8,128)(2,1)}) custom-call(s32[8]{0:T(128)} %select_reduce_fusion.order, f32[8,2]{1,0:T(8,128)} %broadcast_power_fusion.1.old_scale, f32[128,128]{1,0:T(8,128)} %get-tuple-element.7.cosine, f32[128,128]{1,0:T(8,128)} %get-tuple-element.6.sine, ...), custom_call_target="tpu_custom_call" | custom-call | tf_op jit(solution)/shard_map/pallas_call | solution.py:427
  113.0 0.0 copy-start
  113.0 6.8 %convert_element_type.44 = f32[8,2,256,512]{3,2,1,0:T(8,128)} convert(bf16[8,2,256,512]{3,2,1,0:T(8,128)(2,1)} %get-tuple-element.5) | non-fusion elementwise | flops 2097152 | bytes 12582912 | tf_op jit(solution)/shard_map/convert_element_type | solution.py:498
  119.8 0.0 copy-done
  119.8 0.7 copy.16
  (7 shorter events, 0.1 us)
Async XLA Ops:
  113.0 6.8 %copy-start = (bf16[32,2048]{1,0:T(8,128)(2,1)S(1)}, bf16[32,2048]{1,0:T(8,128)(2,1)}, u32[]{:S(2)}) copy-start(bf16[32,2048]{1,0:T(8,128)(2,1)} %get-tuple-element.14) | copy-start | bytes 393220

commit v2 on v1

--- a/solution.py
+++ b/solution.py
@@ -21,11 +21,6 @@
     return centred * lax.rsqrt(variance + epsilon)
 
 
-def decays(head_count, first_head):
-    head_index = jnp.arange(head_count, dtype=jnp.float32) + first_head
-    return 1.0 - jnp.exp2(-5.0 - head_index)
-
-
 MESH = pl.DeviceIdType.MESH
 F32 = jnp.float32
 BF16 = jnp.bfloat16
@@ -38,13 +33,9 @@
 def kernel(
     n,
     m,
-    order,
-    old_scale,
-    cosine,
-    sine,
-    mask,
-    carry,
-    fold,
+    prompt,
+    accepted,
+    slots,
     tokens,
     states,
     w_query,
@@ -202,11 +193,42 @@
         for k in range(1, n):
             send_shard(me, True, lax.rem(me + k, n), k - 1)
 
+    row = lax.broadcasted_iota(jnp.int32, (rows, half), 0)
+    draft_pos = lax.rem(row, draft)
+    start = jnp.zeros((rows, half), jnp.int32)
+    kept = jnp.zeros((rows, half), jnp.int32)
+    for r in range(requests):
+        start = jnp.where(row >= r * draft, prompt[r], start)
+        kept = jnp.where(row >= r * draft, accepted[r], kept)
+    lane = lax.broadcasted_iota(jnp.int32, (rows, half), 1).astype(F32)
+    angles = (start + draft_pos).astype(F32) * jnp.exp(-math.log(10000.0) * lane / half)
+    cos_part, sin_part = jnp.cos(angles), jnp.sin(angles)
+    exponent = (kept - 1 - draft_pos).astype(F32)
+    to = lax.broadcasted_iota(jnp.int32, (rows, rows), 0)
+    source = lax.broadcasted_iota(jnp.int32, (rows, rows), 1)
+    causal = (to // draft == source // draft) & (to >= source)
+    distance = (to - source).astype(F32)
+
+    def log_gamma(h, shape):
+        head = jnp.full(shape, mj * heads + h, jnp.int32).astype(F32)
+        return jnp.log(1.0 - jnp.exp2(-5.0 - head))
+
+    fold, mask, carry = [], [], []
+    for h in range(heads):
+        lg = log_gamma(h, (1, half))
+        weight = jnp.where(exponent >= 0, jnp.exp(jnp.maximum(exponent, 0.0) * lg), 0.0)
+        fold.append(jnp.concatenate([weight, weight], axis=-1))
+        carry.append(jnp.exp((draft_pos.astype(F32) + 1.0) * lg)[:, :1])
+        mask.append(
+            jnp.where(
+                causal, jnp.exp(jnp.maximum(distance, 0.0) * log_gamma(h, (1, rows))), 0.0
+            )
+        )
+
     loads[0].wait()
     for copy in tok_copies:
         copy.wait_recv()
     normed[...] = layer_norm(tok[...].astype(F32).reshape(rows, width)).astype(BF16)
-    cos_part, sin_part = cosine[...], sine[...]
 
     def turned(v):
         front, back = v[:, :half], v[:, half:]
@@ -225,66 +247,31 @@
             (rk.astype(F32) * fold[h]).astype(BF16).reshape(requests, draft, dk)
         )
     loads[3].wait()
-    loads[4].wait()
     for h in range(heads):
         cols = pl.ds(h * dv, dv)
         vals[:, :, cols] = mm(normed[...], wv[:, cols]).astype(BF16).reshape(
             requests, draft, dv
         )
-        g = mm(normed[...], wgr[:, cols])
-        gated[:, cols] = g / (1.0 + jnp.exp(-g))
     loads[5].wait()
 
-    @pl.loop(0, requests)
-    def _(r):
-        here = pl.ds(pl.multiple_of(r * draft, draft), draft)
+    st_copies = []
+
+    def fresh(p):
+        r = 0
+        for q in range(requests):
+            slot = slots[q]
+            place = slot // requests * per_peer + lax.rem(slot, per_peer)
+            r = jnp.where(place == p, q, r)
+        count = jnp.full((1, dv), accepted[r], jnp.int32).astype(F32)
         for h in range(heads):
-            outs[here, h * dv : (h + 1) * dv] = mm(
-                rq[here, h * dk : (h + 1) * dk], st[r, h].astype(BF16)
-            )
-
-    for h in range(heads):
-        cols = pl.ds(h * dk, dk)
-        vcols = pl.ds(h * dv, dv)
-        scores = lax.dot_general(
-            rq[:, cols], rk_h[:, cols], (((1,), (1,)), ((), ())), preferred_element_type=F32
-        )
-        weights = (scores * mask[h]).astype(BF16)
-        out = mm(weights, vals[:, :, vcols].reshape(rows, dv)) + outs[:, vcols] * carry[h]
-        joined[:, vcols] = (layer_norm(out) * gated[:, vcols]).astype(BF16)
-
-    loads[6].wait()
-    step = min(512, width)
-
-    @pl.loop(0, width // step)
-    def _(c):
-        cols = pl.ds(pl.multiple_of(c * step, step), step)
-        part[:, :, cols] = mm(joined[...], wo[:, cols]).astype(BF16).reshape(m, share, step)
-
-    part_copies = mlp_copies(
-        lambda peer: part.at[peer], lambda k: part_in.at[k - 1], part_s, part_r
-    )
-
-    if n == 8:
-        arrived(0)
-        send_shard(flip(2), False, flip(4), 3, (0, 1))
-        arrived(1)
-        send_shard(flip(4), False, flip(2), 3, (2, 3))
-        send_shard(flip(2), False, flip(1), 4)
-        send_shard(flip(4), False, flip(1), 5)
-
-    st_copies = []
-
-    def fresh(p):
-        r = order[p]
-        for h in range(heads):
+            old_scale = jnp.exp(count * log_gamma(h, (1, dv)))
             update = lax.dot_general(
                 ksc[r, :, h * dk : (h + 1) * dk],
                 vals[r, :, h * dv : (h + 1) * dv],
                 (((0,), (0,)), ((), ())),
                 preferred_element_type=F32,
             )
-            send_buf[p, h] = (old_scale[r, h] * st[r, h] + update).astype(BF16)
+            send_buf[p, h] = (old_scale * st[r, h] + update).astype(BF16)
 
     pl.loop(0, requests)(fresh)
     mine = pl.ds(me * per_peer, per_peer)
@@ -302,6 +289,50 @@
         st_copies.append(copy)
     keep = pltpu.make_async_copy(send_buf.at[mine], moved.at[mine], load_sem.at[10])
     keep.start()
+
+    loads[4].wait()
+    for h in range(heads):
+        cols = pl.ds(h * dv, dv)
+        g = mm(normed[...], wgr[:, cols])
+        gated[:, cols] = g / (1.0 + jnp.exp(-g))
+
+    @pl.loop(0, requests)
+    def _(r):
+        here = pl.ds(pl.multiple_of(r * draft, draft), draft)
+        for h in range(heads):
+            outs[here, h * dv : (h + 1) * dv] = mm(
+                rq[here, h * dk : (h + 1) * dk], st[r, h].astype(BF16)
+            )
+
+    for h in range(heads):
+        cols = pl.ds(h * dk, dk)
+        vcols = pl.ds(h * dv, dv)
+        scores = lax.dot_general(
+            rq[:, cols], rk_h[:, cols], (((1,), (1,)), ((), ())), preferred_element_type=F32
+        )
+        weights = (scores * mask[h]).astype(BF16)
+        out = mm(weights, vals[:, :, vcols].reshape(rows, dv)) + outs[:, vcols] * carry[h]
+        joined[:, vcols] = (layer_norm(out) * gated[:, vcols]).astype(BF16)
+
+    loads[6].wait()
+    step = min(512, width)
+
+    @pl.loop(0, width // step)
+    def _(c):
+        cols = pl.ds(pl.multiple_of(c * step, step), step)
+        part[:, :, cols] = mm(joined[...], wo[:, cols]).astype(BF16).reshape(m, share, step)
+
+    part_copies = mlp_copies(
+        lambda peer: part.at[peer], lambda k: part_in.at[k - 1], part_s, part_r
+    )
+
+    if n == 8:
+        arrived(0)
+        send_shard(flip(2), False, flip(4), 3, (0, 1))
+        arrived(1)
+        send_shard(flip(4), False, flip(2), 3, (2, 3))
+        send_shard(flip(2), False, flip(1), 4)
+        send_shard(flip(4), False, flip(1), 5)
 
     total = part[mj].astype(F32)
     for k, copy in enumerate(part_copies):
@@ -385,37 +416,6 @@
     m = lax.axis_size("mlp")
     share, width = tokens.shape
     rows = requests * DRAFT
-    per_peer = requests // n
-    gammas = decays(heads, (lax.axis_index("mlp") * heads).astype(F32))
-    target_pos = owner_slot // requests * per_peer + owner_slot % per_peer
-    ids = jnp.arange(requests, dtype=jnp.int32)
-    order = jnp.sum(jnp.where(target_pos[None, :] == ids[:, None], ids[None, :], 0), axis=1)
-    kept = accepted.astype(F32)
-    old_scale = jnp.power(gammas[None, :], kept[:, None])
-    draft_pos = jnp.arange(DRAFT, dtype=F32)
-    exponent = kept[:, None] - 1.0 - draft_pos[None, :]
-    fold = jnp.where(
-        exponent[None] >= 0,
-        jnp.power(gammas[:, None, None], jnp.maximum(exponent, 0.0)[None]),
-        0.0,
-    ).reshape(heads, rows, 1)
-    row = jnp.arange(rows, dtype=jnp.int32)
-    distance = (row[:, None] - row[None, :]).astype(F32)
-    same = (row[:, None] // DRAFT == row[None, :] // DRAFT) & (distance >= 0)
-    mask = jnp.where(
-        same[None], jnp.power(gammas[:, None, None], jnp.maximum(distance, 0.0)[None]), 0.0
-    )
-    carry = jnp.power(
-        gammas[:, None, None], ((row % DRAFT).astype(F32) + 1.0)[None, :, None]
-    )
-    half = dk // 2
-    frequencies = jnp.exp(-math.log(10000.0) * jnp.arange(half, dtype=F32) / half)
-    positions = (
-        (prompt_lengths[:, None] + jnp.arange(DRAFT, dtype=jnp.int32)[None, :])
-        .astype(F32)
-        .reshape(rows, 1)
-    )
-    angles = positions * frequencies[None, :]
     vmem = pl.BlockSpec(memory_space=pltpu.VMEM)
     smem = pl.BlockSpec(memory_space=pltpu.SMEM)
     hbm = pl.BlockSpec(memory_space=pl.ANY)
@@ -430,7 +430,7 @@
             jax.ShapeDtypeStruct((share, width), BF16),
             jax.ShapeDtypeStruct((requests, heads, dk, dv), BF16),
         ),
-        in_specs=[smem] * 2 + [vmem] * 5 + [hbm] * 10,
+        in_specs=[smem] * 3 + [hbm] * 10,
         out_specs=(vmem, hbm),
         scratch_shapes=[
             v(w_query.shape),
@@ -477,13 +477,9 @@
             collective_id=0, has_side_effects=True, vmem_limit_bytes=60 * 1024 * 1024
         ),
     )(
-        order,
-        old_scale,
-        jnp.cos(angles),
-        jnp.sin(angles),
-        mask,
-        carry,
-        fold,
+        prompt_lengths,
+        accepted,
+        owner_slot,
         tokens,
         cached_states,
         w_query,

time: 122 us -> 131 us (1.074)
  Pallas kernels: 105 us -> 122 us
  other arithmetic: 13.2 us -> 6.77 us
    pallas_call x1, Pallas kernels: 105 us -> 122 us  [per_device(): pl.pallas_call(functools.partial(kernel, n, m), out_shape=(jax.ShapeDtype...]
    select_n x4 -> x0, other arithmetic: 2.59 us -> none  [the longest x1 1.04 us: per_device(): jnp.where(exponent[None] >= 0, jnp.power(gammas[:, None, None], jnp.maxim...]
    convert_element_type x2 -> x0, other arithmetic: 1.39 us -> none  [the longest x1 0.73 us: per_device(): positions = (prompt_lengths[:, None] + jnp.arange(DRAFT, dtype=jnp.int32)...]
where the time goes in v2:
time: 131 us; the launch traced here: 130 us
  Pallas kernels  122 us (93%)
  other arithmetic  6.77 us (5%)
    pallas_call x1, Pallas kernels, per_device(): pl.pallas_call(functools.partial(kernel, n, m), out_shape=(jax.ShapeDtype...  122 us
    convert_element_type x1, other arithmetic, per_device(): return (mixed, moved.astype(F32))  6.77 us

profile of v2, /device:TPU:0, one launch (start us, length us, event | category | flops | bytes accessed | tf_op | source)
XLA Modules:
  0.0 130.3 jit_solution(2365621515530865946)
XLA Ops:
  0.6 122.3 %shard_map.140 = (bf16[32,2048]{1,0:T(8,128)(2,1)}, bf16[8,2,256,512]{3,2,1,0:T(8,128)(2,1)}) custom-call(s32[8]{0:T(128)} %prompt.1, s32[8]{0:T(128)} %accepted.1, s32[8]{0:T(128)} %slots.1, bf16[32,2048]{1,0:T(8,128)(2,1)} %tokens.1, f32[8,2,256,512]{3,2,1,0:T(8,128)} %states.1, bf16[2048,512]{1,0:T(8,128)(2,1)} %w_query.1, bf16[2048,512]{1,0:T(8,128)(2,1)} %w_key.1, ...), custom_call_target="tpu_custom_call" | custom-call | tf_op jit(solution)/shard_map/pallas_call | solution.py:427
  122.9 0.0 copy-start
  122.9 6.8 %convert_element_type.3 = f32[8,2,256,512]{3,2,1,0:T(8,128)} convert(bf16[8,2,256,512]{3,2,1,0:T(8,128)(2,1)} %get-tuple-element.5) | non-fusion elementwise | flops 2097152 | bytes 12582912 | tf_op jit(solution)/shard_map/convert_element_type | solution.py:494
  129.7 0.0 copy-done
  129.7 0.7 copy.16
Async XLA Ops:
  122.9 6.8 %copy-start = (bf16[32,2048]{1,0:T(8,128)(2,1)S(1)}, bf16[32,2048]{1,0:T(8,128)(2,1)}, u32[]{:S(2)}) copy-start(bf16[32,2048]{1,0:T(8,128)(2,1)} %get-tuple-element.8) | copy-start | bytes 393220

commit v3 on v2

--- a/solution.py
+++ b/solution.py
@@ -254,6 +254,50 @@
         )
     loads[5].wait()
 
+    loads[4].wait()
+    for h in range(heads):
+        cols = pl.ds(h * dv, dv)
+        g = mm(normed[...], wgr[:, cols])
+        gated[:, cols] = g / (1.0 + jnp.exp(-g))
+
+    @pl.loop(0, requests)
+    def _(r):
+        here = pl.ds(pl.multiple_of(r * draft, draft), draft)
+        for h in range(heads):
+            outs[here, h * dv : (h + 1) * dv] = mm(
+                rq[here, h * dk : (h + 1) * dk], st[r, h].astype(BF16)
+            )
+
+    for h in range(heads):
+        cols = pl.ds(h * dk, dk)
+        vcols = pl.ds(h * dv, dv)
+        scores = lax.dot_general(
+            rq[:, cols], rk_h[:, cols], (((1,), (1,)), ((), ())), preferred_element_type=F32
+        )
+        weights = (scores * mask[h]).astype(BF16)
+        out = mm(weights, vals[:, :, vcols].reshape(rows, dv)) + outs[:, vcols] * carry[h]
+        joined[:, vcols] = (layer_norm(out) * gated[:, vcols]).astype(BF16)
+
+    loads[6].wait()
+    step = min(512, width)
+
+    @pl.loop(0, width // step)
+    def _(c):
+        cols = pl.ds(pl.multiple_of(c * step, step), step)
+        part[:, :, cols] = mm(joined[...], wo[:, cols]).astype(BF16).reshape(m, share, step)
+
+    part_copies = mlp_copies(
+        lambda peer: part.at[peer], lambda k: part_in.at[k - 1], part_s, part_r
+    )
+
+    if n == 8:
+        arrived(0)
+        send_shard(flip(2), False, flip(4), 3, (0, 1))
+        arrived(1)
+        send_shard(flip(4), False, flip(2), 3, (2, 3))
+        send_shard(flip(2), False, flip(1), 4)
+        send_shard(flip(4), False, flip(1), 5)
+
     st_copies = []
 
     def fresh(p):
@@ -274,6 +318,23 @@
             send_buf[p, h] = (old_scale * st[r, h] + update).astype(BF16)
 
     pl.loop(0, requests)(fresh)
+
+    total = part[mj].astype(F32)
+    for k, copy in enumerate(part_copies):
+        copy.wait_recv()
+        total = total + part_in[k].astype(F32)
+    residual = tok[mj].astype(F32) + total
+    res[...] = residual
+    hid[mj] = layer_norm(residual).astype(BF16)
+    hid_copies = mlp_copies(lambda peer: hid.at[mj], lambda k: hid.at[mj], hid_s, hid_r)
+
+    if n == 8:
+        arrived(3)
+        send_shard(flip(6), False, flip(1), 6)
+        last = (2, 4, 5, 6)
+    else:
+        last = tuple(range(n - 1))
+
     mine = pl.ds(me * per_peer, per_peer)
     for k in range(1, n):
         peer = lax.rem(me + k, n)
@@ -289,66 +350,6 @@
         st_copies.append(copy)
     keep = pltpu.make_async_copy(send_buf.at[mine], moved.at[mine], load_sem.at[10])
     keep.start()
-
-    loads[4].wait()
-    for h in range(heads):
-        cols = pl.ds(h * dv, dv)
-        g = mm(normed[...], wgr[:, cols])
-        gated[:, cols] = g / (1.0 + jnp.exp(-g))
-
-    @pl.loop(0, requests)
-    def _(r):
-        here = pl.ds(pl.multiple_of(r * draft, draft), draft)
-        for h in range(heads):
-            outs[here, h * dv : (h + 1) * dv] = mm(
-                rq[here, h * dk : (h + 1) * dk], st[r, h].astype(BF16)
-            )
-
-    for h in range(heads):
-        cols = pl.ds(h * dk, dk)
-        vcols = pl.ds(h * dv, dv)
-        scores = lax.dot_general(
-            rq[:, cols], rk_h[:, cols], (((1,), (1,)), ((), ())), preferred_element_type=F32
-        )
-        weights = (scores * mask[h]).astype(BF16)
-        out = mm(weights, vals[:, :, vcols].reshape(rows, dv)) + outs[:, vcols] * carry[h]
-        joined[:, vcols] = (layer_norm(out) * gated[:, vcols]).astype(BF16)
-
-    loads[6].wait()
-    step = min(512, width)
-
-    @pl.loop(0, width // step)
-    def _(c):
-        cols = pl.ds(pl.multiple_of(c * step, step), step)
-        part[:, :, cols] = mm(joined[...], wo[:, cols]).astype(BF16).reshape(m, share, step)
-
-    part_copies = mlp_copies(
-        lambda peer: part.at[peer], lambda k: part_in.at[k - 1], part_s, part_r
-    )
-
-    if n == 8:
-        arrived(0)
-        send_shard(flip(2), False, flip(4), 3, (0, 1))
-        arrived(1)
-        send_shard(flip(4), False, flip(2), 3, (2, 3))
-        send_shard(flip(2), False, flip(1), 4)
-        send_shard(flip(4), False, flip(1), 5)
-
-    total = part[mj].astype(F32)
-    for k, copy in enumerate(part_copies):
-        copy.wait_recv()
-        total = total + part_in[k].astype(F32)
-    residual = tok[mj].astype(F32) + total
-    res[...] = residual
-    hid[mj] = layer_norm(residual).astype(BF16)
-    hid_copies = mlp_copies(lambda peer: hid.at[mj], lambda k: hid.at[mj], hid_s, hid_r)
-
-    if n == 8:
-        arrived(3)
-        send_shard(flip(6), False, flip(1), 6)
-        last = (2, 4, 5, 6)
-    else:
-        last = tuple(range(n - 1))
     for copy in hid_copies:
         copy.wait_recv()
     for slot in last:
@@ -394,6 +395,10 @@
         copy.wait_send()
     for copy in w_copies.values():
         copy.wait_send()
+
+
+def widen(x, out):
+    out[...] = x[...].astype(F32)
 
 
 def per_device(
@@ -491,7 +496,15 @@
         w_up,
         w_down,
     )
-    return (mixed, moved.astype(F32))
+    block = pl.BlockSpec((1, 1, dk, dv), lambda r, h: (r, h, 0, 0))
+    new_states = pl.pallas_call(
+        widen,
+        out_shape=jax.ShapeDtypeStruct(cached_states.shape, F32),
+        grid=(requests, heads),
+        in_specs=[block],
+        out_specs=block,
+    )(moved)
+    return (mixed, new_states)
 
 
 def solution(mesh):

time: 131 us -> 118 us (0.901)
  other arithmetic: 6.77 us -> 0 us
  Pallas kernels: 122 us -> 116 us
    pallas_call x1, Pallas kernels: 122 us -> 105 us  [per_device(): pl.pallas_call(functools.partial(kernel, n, m), out_shape=(jax.ShapeDtype...]
    pallas_call x0 -> x1, Pallas kernels: none -> 10.8 us  [per_device(): pl.pallas_call(widen, out_shape=jax.ShapeDtypeStruct(cached_states.shape,...]
    convert_element_type x1 -> x0, other arithmetic: 6.77 us -> none  [per_device(): return (mixed, moved.astype(F32))]
where the time goes in v3:
time: 118 us; the launch traced here: 117 us
  Pallas kernels  116 us (98%)
    pallas_call x1, Pallas kernels, per_device(): pl.pallas_call(functools.partial(kernel, n, m), out_shape=(jax.ShapeDtype...  105 us
    pallas_call x1, Pallas kernels, per_device(): pl.pallas_call(widen, out_shape=jax.ShapeDtypeStruct(cached_states.shape,...  10.8 us

profile of v3, /device:TPU:0, one launch (start us, length us, event | category | flops | bytes accessed | tf_op | source)
XLA Modules:
  0.0 117.3 jit_solution(12638116843599428580)
XLA Ops:
  0.6 105.2 %shard_map.140 = (bf16[32,2048]{1,0:T(8,128)(2,1)}, bf16[8,2,256,512]{3,2,1,0:T(8,128)(2,1)}) custom-call(s32[8]{0:T(128)} %prompt.1, s32[8]{0:T(128)} %accepted.1, s32[8]{0:T(128)} %slots.1, bf16[32,2048]{1,0:T(8,128)(2,1)} %tokens.1, f32[8,2,256,512]{3,2,1,0:T(8,128)} %states.1, bf16[2048,512]{1,0:T(8,128)(2,1)} %w_query.1, bf16[2048,512]{1,0:T(8,128)(2,1)} %w_key.1, ...), custom_call_target="tpu_custom_call" | custom-call | tf_op jit(solution)/shard_map/pallas_call | solution.py:432
  105.8 0.0 copy-start
  105.8 10.8 %shard_map.141 = f32[8,2,256,512]{3,2,1,0:T(8,128)} custom-call(bf16[8,2,256,512]{3,2,1,0:T(8,128)(2,1)} %get-tuple-element.5.x), custom_call_target="tpu_custom_call" | custom-call | tf_op jit(solution)/shard_map/pallas_call | solution.py:500
  116.7 0.0 copy-done
  116.7 0.7 copy.16
Async XLA Ops:
  105.8 10.8 %copy-start = (bf16[32,2048]{1,0:T(8,128)(2,1)S(1)}, bf16[32,2048]{1,0:T(8,128)(2,1)}, u32[]{:S(2)}) copy-start(bf16[32,2048]{1,0:T(8,128)(2,1)} %get-tuple-element.8) | copy-start | bytes 393220

commit v4 on v2

--- a/solution.py
+++ b/solution.py
@@ -74,6 +74,14 @@
     part2,
     part2_in,
     send_buf,
+    hx,
+    hy,
+    sx,
+    sy,
+    rx,
+    ry,
+    og,
+    ou,
     load_sem,
     tok_s,
     tok_r,
@@ -87,6 +95,8 @@
     w_r,
     st_s,
     st_r,
+    x_s,
+    x_r,
 ):
     me = lax.axis_index("req")
     mj = lax.axis_index("mlp")
@@ -147,36 +157,40 @@
     tok_copies = mlp_copies(lambda peer: tokens, lambda k: tok.at[mj], tok_s, tok_r)
 
     cut = w_down.shape[0] // 2
-    first = pl.ds(0, cut)
-    second = pl.ds(cut, cut)
-
-    def pieces(owner, own):
-        if own:
-            source = (w_gate, w_down.at[first], w_up, w_down.at[second])
-        else:
-            source = None
-        there = (fg.at[owner], fd.at[owner, first], fu.at[owner], fd.at[owner, second])
-        return source or there, there
+    edge = w_gate.shape[1] // 2
+    both = pl.ds(0, w_gate.shape[0])
+    cut_of = {
+        "g": (w_gate, fg, ()),
+        "u": (w_up, fu, ()),
+        "ga": (w_gate, fg, (both, pl.ds(0, edge))),
+        "gb": (w_gate, fg, (both, pl.ds(edge, edge))),
+        "ua": (w_up, fu, (both, pl.ds(0, edge))),
+        "ub": (w_up, fu, (both, pl.ds(edge, edge))),
+        "d0": (w_down, fd, (pl.ds(0, cut),)),
+        "d1": (w_down, fd, (pl.ds(cut, cut),)),
+    }
 
     w_copies = {}
 
-    def send_shard(owner, own, peer, slot, which=(0, 1, 2, 3)):
-        source, there = pieces(owner, own)
-        for i in which:
+    def send_shard(owner, own, peer, slot, names=("g", "u", "d0", "d1"), at=0):
+        for i, name in enumerate(names):
+            given, held, where = cut_of[name]
+            there = held.at[(owner,) + where]
             copy = pltpu.make_async_remote_copy(
-                src_ref=source[i],
-                dst_ref=there[i],
-                send_sem=w_s.at[slot, i],
-                recv_sem=w_r.at[slot, i],
+                src_ref=(given.at[where] if where else given) if own else there,
+                dst_ref=there,
+                send_sem=w_s.at[slot, at + i],
+                recv_sem=w_r.at[slot, at + i],
                 device_id={"req": peer},
                 device_id_type=MESH,
             )
             copy.start()
-            w_copies[slot, i] = copy
-
-    def arrived(slot, which=(0, 1, 2, 3)):
-        for i in which:
-            w_copies[slot, i].wait_recv()
+            w_copies[slot, at + i] = copy
+
+    def arrived(slot):
+        for (at, _), copy in w_copies.items():
+            if at == slot:
+                copy.wait_recv()
 
     def flip(bits):
         out = me
@@ -186,8 +200,10 @@
         return out
 
     if n == 8:
-        send_shard(me, True, flip(2), 0)
-        send_shard(me, True, flip(4), 1)
+        side_x = ("gb", "ub", "d0", "d1")
+        side_y = ("ga", "ua", "d0", "d1")
+        send_shard(me, True, flip(2), 0, side_x)
+        send_shard(me, True, flip(4), 1, side_y)
         send_shard(me, True, flip(1), 2)
     else:
         for k in range(1, n):
@@ -275,18 +291,25 @@
 
     pl.loop(0, requests)(fresh)
     mine = pl.ds(me * per_peer, per_peer)
-    for k in range(1, n):
-        peer = lax.rem(me + k, n)
+
+    def send_states(peer, slot):
         copy = pltpu.make_async_remote_copy(
             src_ref=send_buf.at[pl.ds(peer * per_peer, per_peer)],
             dst_ref=moved.at[mine],
-            send_sem=st_s.at[k - 1],
-            recv_sem=st_r.at[k - 1],
+            send_sem=st_s.at[slot],
+            recv_sem=st_r.at[slot],
             device_id={"req": peer},
             device_id_type=MESH,
         )
         copy.start()
         st_copies.append(copy)
+
+    if n == 8:
+        for bits in (2, 4, 6, 3, 5, 1):
+            send_states(flip(bits), bits - 1)
+    else:
+        for k in range(1, n):
+            send_states(lax.rem(me + k, n), k - 1)
     keep = pltpu.make_async_copy(send_buf.at[mine], moved.at[mine], load_sem.at[10])
     keep.start()
 
@@ -328,11 +351,11 @@
 
     if n == 8:
         arrived(0)
-        send_shard(flip(2), False, flip(4), 3, (0, 1))
+        send_shard(flip(2), False, flip(4), 3, ("d0",))
         arrived(1)
-        send_shard(flip(4), False, flip(2), 3, (2, 3))
-        send_shard(flip(2), False, flip(1), 4)
-        send_shard(flip(4), False, flip(1), 5)
+        send_shard(flip(4), False, flip(2), 3, ("d1",), 1)
+        send_shard(flip(2), False, flip(1), 4, side_x)
+        send_shard(flip(4), False, flip(1), 5, side_y)
 
     total = part[mj].astype(F32)
     for k, copy in enumerate(part_copies):
@@ -343,33 +366,101 @@
     hid[mj] = layer_norm(residual).astype(BF16)
     hid_copies = mlp_copies(lambda peer: hid.at[mj], lambda k: hid.at[mj], hid_s, hid_r)
 
-    if n == 8:
-        arrived(3)
-        send_shard(flip(6), False, flip(1), 6)
-        last = (2, 4, 5, 6)
-    else:
-        last = tuple(range(n - 1))
     for copy in hid_copies:
         copy.wait_recv()
-    for slot in last:
-        arrived(slot)
-    for copy in loads[7:]:
-        copy.wait()
 
     rows_in = fg.shape[1]
     inner = fg.shape[2]
-    tile = min(256, inner)
-
-    @pl.loop(0, inner // tile)
-    def _(c):
-        cols = pl.ds(pl.multiple_of(c * tile, tile), tile)
-        g = jnp.zeros((rows, tile), F32)
-        u = jnp.zeros((rows, tile), F32)
-        for i in range(n):
-            a = hid[:, :, i * rows_in : (i + 1) * rows_in].reshape(rows, rows_in)
-            g = g + mm(a, fg[i, :, cols])
-            u = u + mm(a, fu[i, :, cols])
-        hs[:, cols] = (g / (1.0 + jnp.exp(-g)) * u).astype(BF16)
+    tile = min(256, inner // 2)
+    if n == 8:
+        pair = 2 * rows_in
+
+        def lanes(i):
+            return pl.ds(pl.multiple_of(i // 2 * pair, pair), pair)
+
+        def exchange(source, there, slot, peer):
+            copy = pltpu.make_async_remote_copy(
+                src_ref=source,
+                dst_ref=there,
+                send_sem=x_s.at[slot],
+                recv_sem=x_r.at[slot],
+                device_id={"req": peer},
+                device_id_type=MESH,
+            )
+            copy.start()
+            return copy
+
+        near, far = pl.ds(0, pair), pl.ds(pair, pair)
+        x_copies = [
+            exchange(hid.at[:, :, lanes(flip(2))], hx.at[:, :, near], 0, flip(2)),
+            exchange(hid.at[:, :, lanes(flip(6))], hx.at[:, :, far], 1, flip(2)),
+            exchange(hid.at[:, :, lanes(flip(4))], hy.at[:, :, near], 2, flip(4)),
+            exchange(hid.at[:, :, lanes(flip(6))], hy.at[:, :, far], 3, flip(4)),
+        ]
+        for slot in (2, 4, 5):
+            arrived(slot)
+        for copy in loads[7:]:
+            copy.wait()
+
+        def partial_sums(other, start, mate, theirs):
+            @pl.loop(0, edge // tile)
+            def _(c):
+                cols = pl.ds(pl.multiple_of(start + c * tile, tile), tile)
+                g = jnp.zeros((2 * rows, tile), F32)
+                u = jnp.zeros((2 * rows, tile), F32)
+                for place, base in ((near, me // 2), (far, mate // 2)):
+                    a = jnp.concatenate(
+                        [
+                            hid[:, :, lanes(2 * base)].reshape(rows, pair),
+                            other[:, :, place].reshape(rows, pair),
+                        ],
+                        axis=0,
+                    )
+                    for odd in range(2):
+                        piece = a[:, odd * rows_in : (odd + 1) * rows_in]
+                        g = g + mm(piece, fg[2 * base + odd, :, cols])
+                        u = u + mm(piece, fu[2 * base + odd, :, cols])
+                og[:, cols] = g[:rows]
+                ou[:, cols] = u[:rows]
+                here = pl.ds(pl.multiple_of(c * tile, tile), tile)
+                theirs[0, :, here] = g[rows:].astype(BF16)
+                theirs[1, :, here] = u[rows:].astype(BF16)
+
+        x_copies[0].wait_recv()
+        x_copies[1].wait_recv()
+        partial_sums(hx, 0, flip(4), sx)
+        x_copies.append(exchange(sx, rx, 4, flip(2)))
+        x_copies[2].wait_recv()
+        x_copies[3].wait_recv()
+        partial_sums(hy, edge, flip(2), sy)
+        x_copies.append(exchange(sy, ry, 5, flip(4)))
+        send_states(flip(7), 6)
+        arrived(3)
+        send_shard(flip(6), False, flip(1), 6, ("d0", "d1"))
+        for copy, got, start in ((x_copies[4], rx, 0), (x_copies[5], ry, edge)):
+            copy.wait_recv()
+            cols = pl.ds(start, edge)
+            g = og[:, cols] + got[0].astype(F32)
+            u = ou[:, cols] + got[1].astype(F32)
+            hs[:, cols] = (g / (1.0 + jnp.exp(-g)) * u).astype(BF16)
+        arrived(6)
+    else:
+        x_copies = []
+        for slot in range(n - 1):
+            arrived(slot)
+        for copy in loads[7:]:
+            copy.wait()
+
+        @pl.loop(0, inner // tile)
+        def _(c):
+            cols = pl.ds(pl.multiple_of(c * tile, tile), tile)
+            g = jnp.zeros((rows, tile), F32)
+            u = jnp.zeros((rows, tile), F32)
+            for i in range(n):
+                a = hid[:, :, i * rows_in : (i + 1) * rows_in].reshape(rows, rows_in)
+                g = g + mm(a, fg[i, :, cols])
+                u = u + mm(a, fu[i, :, cols])
+            hs[:, cols] = (g / (1.0 + jnp.exp(-g)) * u).astype(BF16)
 
     wide = fd.shape[2]
 
@@ -390,7 +481,7 @@
     keep.wait()
     for copy in st_copies:
         copy.wait()
-    for copy in tok_copies + part_copies + hid_copies + part2_copies:
+    for copy in tok_copies + part_copies + hid_copies + part2_copies + x_copies:
         copy.wait_send()
     for copy in w_copies.values():
         copy.wait_send()
@@ -459,6 +550,14 @@
             v((m, share, width)),
             v((m - 1, share, width)),
             v(cached_states.shape),
+            v((m, share, 4 * w_gate.shape[0])),
+            v((m, share, 4 * w_gate.shape[0])),
+            v((2, rows, w_gate.shape[1] // 2)),
+            v((2, rows, w_gate.shape[1] // 2)),
+            v((2, rows, w_gate.shape[1] // 2)),
+            v((2, rows, w_gate.shape[1] // 2)),
+            v((rows, w_gate.shape[1]), F32),
+            v((rows, w_gate.shape[1]), F32),
             dma((11,)),
             dma((m - 1,)),
             dma((m - 1,)),
@@ -472,6 +571,8 @@
             dma((n - 1, 4)),
             dma((n - 1,)),
             dma((n - 1,)),
+            dma((6,)),
+            dma((6,)),
         ],
         compiler_params=pltpu.CompilerParams(
             collective_id=0, has_side_effects=True, vmem_limit_bytes=60 * 1024 * 1024

time: 131 us -> 113 us (0.86)
  Pallas kernels: 122 us -> 105 us
    pallas_call x1, Pallas kernels: 122 us -> 105 us  [per_device(): pl.pallas_call(functools.partial(kernel, n, m), out_shape=(jax.ShapeDtype...]
where the time goes in v4:
time: 113 us
  Pallas kernels  105 us (93%)
  other arithmetic  6.77 us (6%)
    pallas_call x1, Pallas kernels, per_device(): pl.pallas_call(functools.partial(kernel, n, m), out_shape=(jax.ShapeDtype...  105 us
    convert_element_type x1, other arithmetic, per_device(): return (mixed, moved.astype(F32))  6.77 us

profile of v4, /device:TPU:0, one launch (start us, length us, event | category | flops | bytes accessed | tf_op | source)
XLA Modules:
  0.0 112.6 jit_solution(17256230852284289300)
XLA Ops:
  0.6 104.5 %shard_map.140 = (bf16[32,2048]{1,0:T(8,128)(2,1)}, bf16[8,2,256,512]{3,2,1,0:T(8,128)(2,1)}) custom-call(s32[8]{0:T(128)} %prompt.1, s32[8]{0:T(128)} %accepted.1, s32[8]{0:T(128)} %slots.1, bf16[32,2048]{1,0:T(8,128)(2,1)} %tokens.1, f32[8,2,256,512]{3,2,1,0:T(8,128)} %states.1, bf16[2048,512]{1,0:T(8,128)(2,1)} %w_query.1, bf16[2048,512]{1,0:T(8,128)(2,1)} %w_key.1, ...), custom_call_target="tpu_custom_call" | custom-call | tf_op jit(solution)/shard_map/pallas_call | solution.py:518
  105.2 0.0 copy-start
  105.2 6.8 %convert_element_type.3 = f32[8,2,256,512]{3,2,1,0:T(8,128)} convert(bf16[8,2,256,512]{3,2,1,0:T(8,128)(2,1)} %get-tuple-element.5) | non-fusion elementwise | flops 2097152 | bytes 12582912 | tf_op jit(solution)/shard_map/convert_element_type | solution.py:595
  112.0 0.0 copy-done
  112.0 0.7 copy.16
Async XLA Ops:
  105.2 6.8 %copy-start = (bf16[32,2048]{1,0:T(8,128)(2,1)S(1)}, bf16[32,2048]{1,0:T(8,128)(2,1)}, u32[]{:S(2)}) copy-start(bf16[32,2048]{1,0:T(8,128)(2,1)} %get-tuple-element.8) | copy-start | bytes 393220

commit v5 on v4

--- a/solution.py
+++ b/solution.py
@@ -136,7 +136,7 @@
 
     pl.semaphore_wait(barrier, n + m - 2)
 
-    def mlp_copies(pick, dst, s, r):
+    def mlp_copies(pick, dst, s, r, base=0):
         copies = []
         for k in range(1, m):
             peer = lax.rem(mj + k, m)
@@ -144,8 +144,8 @@
                 pltpu.make_async_remote_copy(
                     src_ref=pick(peer),
                     dst_ref=dst(k),
-                    send_sem=s.at[k - 1],
-                    recv_sem=r.at[k - 1],
+                    send_sem=s.at[base + k - 1],
+                    recv_sem=r.at[base + k - 1],
                     device_id={"mlp": peer},
                     device_id_type=MESH,
                 )
@@ -338,16 +338,27 @@
         joined[:, vcols] = (layer_norm(out) * gated[:, vcols]).astype(BF16)
 
     loads[6].wait()
-    step = min(512, width)
-
-    @pl.loop(0, width // step)
-    def _(c):
-        cols = pl.ds(pl.multiple_of(c * step, step), step)
-        part[:, :, cols] = mm(joined[...], wo[:, cols]).astype(BF16).reshape(m, share, step)
-
-    part_copies = mlp_copies(
-        lambda peer: part.at[peer], lambda k: part_in.at[k - 1], part_s, part_r
-    )
+    step = min(512, width // 2)
+
+    middle = width // 2
+    part_copies = []
+    for side in range(2):
+
+        @pl.loop(0, middle // step)
+        def _(c):
+            cols = pl.ds(pl.multiple_of(side * middle + c * step, step), step)
+            part[:, :, cols] = (
+                mm(joined[...], wo[:, cols]).astype(BF16).reshape(m, share, step)
+            )
+
+        span = pl.ds(side * middle, middle)
+        part_copies += mlp_copies(
+            lambda peer: part.at[peer, :, span],
+            lambda k: part_in.at[k - 1, :, span],
+            part_s,
+            part_r,
+            side * (m - 1),
+        )
 
     if n == 8:
         arrived(0)
@@ -358,16 +369,14 @@
         send_shard(flip(4), False, flip(1), 5, side_y)
 
     total = part[mj].astype(F32)
-    for k, copy in enumerate(part_copies):
+    for copy in part_copies:
         copy.wait_recv()
+    for k in range(m - 1):
         total = total + part_in[k].astype(F32)
     residual = tok[mj].astype(F32) + total
     res[...] = residual
     hid[mj] = layer_norm(residual).astype(BF16)
     hid_copies = mlp_copies(lambda peer: hid.at[mj], lambda k: hid.at[mj], hid_s, hid_r)
-
-    for copy in hid_copies:
-        copy.wait_recv()
 
     rows_in = fg.shape[1]
     inner = fg.shape[2]
@@ -391,12 +400,21 @@
             return copy
 
         near, far = pl.ds(0, pair), pl.ds(pair, pair)
-        x_copies = [
-            exchange(hid.at[:, :, lanes(flip(2))], hx.at[:, :, near], 0, flip(2)),
-            exchange(hid.at[:, :, lanes(flip(6))], hx.at[:, :, far], 1, flip(2)),
-            exchange(hid.at[:, :, lanes(flip(4))], hy.at[:, :, near], 2, flip(4)),
-            exchange(hid.at[:, :, lanes(flip(6))], hy.at[:, :, far], 3, flip(4)),
-        ]
+        to_x, to_y = [], []
+        for k in range(m):
+            if k > 0:
+                hid_copies[k - 1].wait_recv()
+            came = lax.rem(mj + m - k, m)
+            at = 2 + 4 * k
+            chunk = hid.at[came]
+            to_x += [
+                exchange(chunk.at[:, lanes(flip(2))], hx.at[came, :, near], at, flip(2)),
+                exchange(chunk.at[:, lanes(flip(6))], hx.at[came, :, far], at + 1, flip(2)),
+            ]
+            to_y += [
+                exchange(chunk.at[:, lanes(flip(4))], hy.at[came, :, near], at + 2, flip(4)),
+                exchange(chunk.at[:, lanes(flip(6))], hy.at[came, :, far], at + 3, flip(4)),
+            ]
         for slot in (2, 4, 5):
             arrived(slot)
         for copy in loads[7:]:
@@ -426,18 +444,19 @@
                 theirs[0, :, here] = g[rows:].astype(BF16)
                 theirs[1, :, here] = u[rows:].astype(BF16)
 
-        x_copies[0].wait_recv()
-        x_copies[1].wait_recv()
+        for copy in to_x:
+            copy.wait_recv()
         partial_sums(hx, 0, flip(4), sx)
-        x_copies.append(exchange(sx, rx, 4, flip(2)))
-        x_copies[2].wait_recv()
-        x_copies[3].wait_recv()
+        sum_x = exchange(sx, rx, 0, flip(2))
+        for copy in to_y:
+            copy.wait_recv()
         partial_sums(hy, edge, flip(2), sy)
-        x_copies.append(exchange(sy, ry, 5, flip(4)))
+        sum_y = exchange(sy, ry, 1, flip(4))
+        x_copies = to_x + to_y + [sum_x, sum_y]
         send_states(flip(7), 6)
         arrived(3)
         send_shard(flip(6), False, flip(1), 6, ("d0", "d1"))
-        for copy, got, start in ((x_copies[4], rx, 0), (x_copies[5], ry, edge)):
+        for copy, got, start in ((sum_x, rx, 0), (sum_y, ry, edge)):
             copy.wait_recv()
             cols = pl.ds(start, edge)
             g = og[:, cols] + got[0].astype(F32)
@@ -446,6 +465,8 @@
         arrived(6)
     else:
         x_copies = []
+        for copy in hid_copies:
+            copy.wait_recv()
         for slot in range(n - 1):
             arrived(slot)
         for copy in loads[7:]:
@@ -464,17 +485,26 @@
 
     wide = fd.shape[2]
 
-    @pl.loop(0, n)
-    def _(i):
-        cols = pl.ds(pl.multiple_of(i * wide, wide), wide)
-        part2[:, :, cols] = mm(hs[...], fd[i]).astype(BF16).reshape(m, share, wide)
-
-    part2_copies = mlp_copies(
-        lambda peer: part2.at[peer], lambda k: part2_in.at[k - 1], part2_s, part2_r
-    )
+    part2_copies = []
+    for side in range(2):
+
+        @pl.loop(side * n // 2, (side + 1) * n // 2)
+        def _(i):
+            cols = pl.ds(pl.multiple_of(i * wide, wide), wide)
+            part2[:, :, cols] = mm(hs[...], fd[i]).astype(BF16).reshape(m, share, wide)
+
+        span = pl.ds(side * middle, middle)
+        part2_copies += mlp_copies(
+            lambda peer: part2.at[peer, :, span],
+            lambda k: part2_in.at[k - 1, :, span],
+            part2_s,
+            part2_r,
+            side * (m - 1),
+        )
     total = part2[mj].astype(F32)
-    for k, copy in enumerate(part2_copies):
+    for copy in part2_copies:
         copy.wait_recv()
+    for k in range(m - 1):
         total = total + part2_in[k].astype(F32)
     mixed[...] = (res[...] + total).astype(BF16)
 
@@ -561,18 +591,18 @@
             dma((11,)),
             dma((m - 1,)),
             dma((m - 1,)),
+            dma((2 * (m - 1),)),
+            dma((2 * (m - 1),)),
             dma((m - 1,)),
             dma((m - 1,)),
-            dma((m - 1,)),
-            dma((m - 1,)),
-            dma((m - 1,)),
-            dma((m - 1,)),
+            dma((2 * (m - 1),)),
+            dma((2 * (m - 1),)),
             dma((n - 1, 4)),
             dma((n - 1, 4)),
             dma((n - 1,)),
             dma((n - 1,)),
-            dma((6,)),
-            dma((6,)),
+            dma((2 + 4 * m,)),
+            dma((2 + 4 * m,)),
         ],
         compiler_params=pltpu.CompilerParams(
             collective_id=0, has_side_effects=True, vmem_limit_bytes=60 * 1024 * 1024

time: 113 us -> 113 us (level)
  no operation moved by 1% of the time
where the time goes in v5:
time: 113 us; the launch traced here: 112 us
  Pallas kernels  104 us (92%)
  other arithmetic  6.77 us (6%)
    pallas_call x1, Pallas kernels, per_device(): pl.pallas_call(functools.partial(kernel, n, m), out_shape=(jax.ShapeDtype...  104 us
    convert_element_type x1, other arithmetic, per_device(): return (mixed, moved.astype(F32))  6.77 us

profile of v5, /device:TPU:0, one launch (start us, length us, event | category | flops | bytes accessed | tf_op | source)
XLA Modules:
  0.0 112.1 jit_solution(17107177366937574767)
XLA Ops:
  0.6 104.0 %shard_map.140 = (bf16[32,2048]{1,0:T(8,128)(2,1)}, bf16[8,2,256,512]{3,2,1,0:T(8,128)(2,1)}) custom-call(s32[8]{0:T(128)} %prompt.1, s32[8]{0:T(128)} %accepted.1, s32[8]{0:T(128)} %slots.1, bf16[32,2048]{1,0:T(8,128)(2,1)} %tokens.1, f32[8,2,256,512]{3,2,1,0:T(8,128)} %states.1, bf16[2048,512]{1,0:T(8,128)(2,1)} %w_query.1, bf16[2048,512]{1,0:T(8,128)(2,1)} %w_key.1, ...), custom_call_target="tpu_custom_call" | custom-call | tf_op jit(solution)/shard_map/pallas_call | solution.py:548
  104.6 0.0 copy-start
  104.6 6.8 %convert_element_type.3 = f32[8,2,256,512]{3,2,1,0:T(8,128)} convert(bf16[8,2,256,512]{3,2,1,0:T(8,128)(2,1)} %get-tuple-element.5) | non-fusion elementwise | flops 2097152 | bytes 12582912 | tf_op jit(solution)/shard_map/convert_element_type | solution.py:625
  111.4 0.0 copy-done
  111.4 0.7 copy.16
Async XLA Ops:
  104.6 6.8 %copy-start = (bf16[32,2048]{1,0:T(8,128)(2,1)S(1)}, bf16[32,2048]{1,0:T(8,128)(2,1)}, u32[]{:S(2)}) copy-start(bf16[32,2048]{1,0:T(8,128)(2,1)} %get-tuple-element.8) | copy-start | bytes 393220

commit v6 on v5

--- a/solution.py
+++ b/solution.py
@@ -415,6 +415,7 @@
                 exchange(chunk.at[:, lanes(flip(4))], hy.at[came, :, near], at + 2, flip(4)),
                 exchange(chunk.at[:, lanes(flip(6))], hy.at[came, :, far], at + 3, flip(4)),
             ]
+        send_states(flip(7), 6)
         for slot in (2, 4, 5):
             arrived(slot)
         for copy in loads[7:]:
@@ -453,7 +454,6 @@
         partial_sums(hy, edge, flip(2), sy)
         sum_y = exchange(sy, ry, 1, flip(4))
         x_copies = to_x + to_y + [sum_x, sum_y]
-        send_states(flip(7), 6)
         arrived(3)
         send_shard(flip(6), False, flip(1), 6, ("d0", "d1"))
         for copy, got, start in ((sum_x, rx, 0), (sum_y, ry, edge)):
@@ -515,6 +515,24 @@
         copy.wait_send()
     for copy in w_copies.values():
         copy.wait_send()
+
+
+def widen(x, rows_in, out, rows_out, narrow, wide, in_sem, out_sem, row_sem):
+    through = pltpu.make_async_copy(rows_in, rows_out, row_sem.at[0])
+    through.start()
+    count = x.shape[0]
+    reads, writes = [], []
+    for r in range(count):
+        reads.append(pltpu.make_async_copy(x.at[r], narrow.at[r], in_sem.at[r]))
+        reads[r].start()
+    for r in range(count):
+        reads[r].wait()
+        wide[r] = narrow[r].astype(F32)
+        writes.append(pltpu.make_async_copy(wide.at[r], out.at[r], out_sem.at[r]))
+        writes[r].start()
+    through.wait()
+    for copy in writes:
+        copy.wait()
 
 
 def per_device(
@@ -622,7 +640,24 @@
         w_up,
         w_down,
     )
-    return (mixed, moved.astype(F32))
+    mixed, new_states = pl.pallas_call(
+        widen,
+        out_shape=(
+            jax.ShapeDtypeStruct(mixed.shape, BF16),
+            jax.ShapeDtypeStruct(moved.shape, F32),
+        )[::-1],
+        in_specs=[hbm] * 2,
+        out_specs=(hbm, hbm),
+        scratch_shapes=[
+            v(moved.shape),
+            v(moved.shape, F32),
+            dma((requests,)),
+            dma((requests,)),
+            dma((1,)),
+        ],
+        compiler_params=pltpu.CompilerParams(vmem_limit_bytes=32 * 1024 * 1024),
+    )(moved, mixed)[::-1]
+    return (mixed, new_states)
 
 
 def solution(mesh):

time: 113 us -> 116 us (1.027)
  Pallas kernels: 104 us -> 112 us
  other arithmetic: 6.77 us -> 0 us
  local copies, waits for them, and re-layouts: 0.66 us -> 3.08 us
    convert_element_type x1 -> x0, other arithmetic: 6.77 us -> none  [per_device(): return (mixed, moved.astype(F32))]
    pallas_call x1, Pallas kernels: 104 us -> 108 us  [per_device(): pl.pallas_call(functools.partial(kernel, n, m), out_shape=(jax.ShapeDtype...]
    pallas_call x0 -> x1, Pallas kernels: none -> 3.8 us  [per_device(): pl.pallas_call(widen, out_shape=(jax.ShapeDtypeStruct(mixed.shape, BF16),...]
    unnamed x3 -> x4, local copies, waits for them, and re-layouts: 0.66 us -> 3.08 us
where the time goes in v6:
time: 116 us
  Pallas kernels  112 us (97%)
  local copies, waits for them, and re-layouts  3.08 us (3%)
    pallas_call x1, Pallas kernels, per_device(): pl.pallas_call(functools.partial(kernel, n, m), out_shape=(jax.ShapeDtype...  108 us
    pallas_call x1, Pallas kernels, per_device(): pl.pallas_call(widen, out_shape=(jax.ShapeDtypeStruct(mixed.shape, BF16),...  3.8 us
    unnamed x4, local copies, waits for them, and re-layouts  3.08 us

profile of v6, /device:TPU:0, one launch (start us, length us, event | category | flops | bytes accessed | tf_op | source)
XLA Modules:
  0.0 115.9 jit_solution(12160755463211390009)
XLA Ops:
  0.6 108.4 %shard_map.140 = (bf16[32,2048]{1,0:T(8,128)(2,1)}, bf16[8,2,256,512]{3,2,1,0:T(8,128)(2,1)}) custom-call(s32[8]{0:T(128)} %prompt.1, s32[8]{0:T(128)} %accepted.1, s32[8]{0:T(128)} %slots.1, bf16[32,2048]{1,0:T(8,128)(2,1)} %tokens.1, f32[8,2,256,512]{3,2,1,0:T(8,128)} %states.1, bf16[2048,512]{1,0:T(8,128)(2,1)} %w_query.1, bf16[2048,512]{1,0:T(8,128)(2,1)} %w_key.1, ...), custom_call_target="tpu_custom_call" | custom-call | tf_op jit(solution)/shard_map/pallas_call | solution.py:566
  109.0 0.0 copy-start
  109.1 2.2 %copy-done = bf16[8,2,256,512]{3,2,1,0:T(8,128)(2,1)S(1)} copy-done((bf16[8,2,256,512]{3,2,1,0:T(8,128)(2,1)S(1)}, bf16[8,2,256,512]{3,2,1,0:T(8,128)(2,1)}, u32[]{:S(2)}) %copy-start) | copy-done | bytes 4194328
  111.2 0.0 copy-start.1
  111.2 0.9 copy-done.1
  112.1 3.8 %shard_map.141 = (f32[8,2,256,512]{3,2,1,0:T(8,128)}, bf16[32,2048]{1,0:T(8,128)(2,1)}) custom-call(bf16[8,2,256,512]{3,2,1,0:T(8,128)(2,1)S(1)} %copy-done, bf16[32,2048]{1,0:T(8,128)(2,1)S(1)} %copy-done.1), custom_call_target="tpu_custom_call" | custom-call | tf_op jit(solution)/shard_map/pallas_call | solution.py:643
Async XLA Ops:
  109.0 2.2 %copy-start = (bf16[8,2,256,512]{3,2,1,0:T(8,128)(2,1)S(1)}, bf16[8,2,256,512]{3,2,1,0:T(8,128)(2,1)}, u32[]{:S(2)}) copy-start(bf16[8,2,256,512]{3,2,1,0:T(8,128)(2,1)} %get-tuple-element.6.x) | copy-start | bytes 12582916
  111.2 0.9 copy-start.1

commit v7 on v6

--- a/solution.py
+++ b/solution.py
@@ -292,10 +292,10 @@
     pl.loop(0, requests)(fresh)
     mine = pl.ds(me * per_peer, per_peer)
 
-    def send_states(peer, slot):
+    def send_states(peer, slot, keys=pl.ds(0, dk)):
         copy = pltpu.make_async_remote_copy(
-            src_ref=send_buf.at[pl.ds(peer * per_peer, per_peer)],
-            dst_ref=moved.at[mine],
+            src_ref=send_buf.at[pl.ds(peer * per_peer, per_peer), :, keys],
+            dst_ref=moved.at[mine, :, keys],
             send_sem=st_s.at[slot],
             recv_sem=st_r.at[slot],
             device_id={"req": peer},
@@ -415,7 +415,7 @@
                 exchange(chunk.at[:, lanes(flip(4))], hy.at[came, :, near], at + 2, flip(4)),
                 exchange(chunk.at[:, lanes(flip(6))], hy.at[came, :, far], at + 3, flip(4)),
             ]
-        send_states(flip(7), 6)
+        send_states(flip(7), 6, pl.ds(0, half))
         for slot in (2, 4, 5):
             arrived(slot)
         for copy in loads[7:]:
@@ -453,6 +453,7 @@
             copy.wait_recv()
         partial_sums(hy, edge, flip(2), sy)
         sum_y = exchange(sy, ry, 1, flip(4))
+        send_states(flip(7), 7, pl.ds(half, half))
         x_copies = to_x + to_y + [sum_x, sum_y]
         arrived(3)
         send_shard(flip(6), False, flip(1), 6, ("d0", "d1"))
@@ -617,8 +618,8 @@
             dma((2 * (m - 1),)),
             dma((n - 1, 4)),
             dma((n - 1, 4)),
-            dma((n - 1,)),
-            dma((n - 1,)),
+            dma((n,)),
+            dma((n,)),
             dma((2 + 4 * m,)),
             dma((2 + 4 * m,)),
         ],
@@ -655,7 +656,7 @@
             dma((requests,)),
             dma((1,)),
         ],
-        compiler_params=pltpu.CompilerParams(vmem_limit_bytes=32 * 1024 * 1024),
+        compiler_params=pltpu.CompilerParams(vmem_limit_bytes=60 * 1024 * 1024),
     )(moved, mixed)[::-1]
     return (mixed, new_states)
 

time: 116 us -> 109 us (0.940)
  local copies, waits for them, and re-layouts: 3.08 us -> 0 us
  Pallas kernels: 112 us -> 109 us
    pallas_call x1, Pallas kernels: 108 us -> 103 us  [per_device(): pl.pallas_call(functools.partial(kernel, n, m), out_shape=(jax.ShapeDtype...]
    unnamed x4 -> x0, local copies, waits for them, and re-layouts: 3.08 us -> none
    pallas_call x1, Pallas kernels: 3.8 us -> 5.24 us  [per_device(): pl.pallas_call(widen, out_shape=(jax.ShapeDtypeStruct(mixed.shape, BF16),...]
where the time goes in v7:
time: 109 us
  Pallas kernels  109 us (100%)
    pallas_call x1, Pallas kernels, per_device(): pl.pallas_call(functools.partial(kernel, n, m), out_shape=(jax.ShapeDtype...  103 us
    pallas_call x1, Pallas kernels, per_device(): pl.pallas_call(widen, out_shape=(jax.ShapeDtypeStruct(mixed.shape, BF16),...  5.24 us

profile of v7, /device:TPU:0, one launch (start us, length us, event | category | flops | bytes accessed | tf_op | source)
XLA Modules:
  0.0 109.2 jit_solution(17724647186009443891)
XLA Ops:
  0.6 103.4 %shard_map.140 = (bf16[32,2048]{1,0:T(8,128)(2,1)}, bf16[8,2,256,512]{3,2,1,0:T(8,128)(2,1)}) custom-call(s32[8]{0:T(128)} %prompt.1, s32[8]{0:T(128)} %accepted.1, s32[8]{0:T(128)} %slots.1, bf16[32,2048]{1,0:T(8,128)(2,1)} %tokens.1, f32[8,2,256,512]{3,2,1,0:T(8,128)} %states.1, bf16[2048,512]{1,0:T(8,128)(2,1)} %w_query.1, bf16[2048,512]{1,0:T(8,128)(2,1)} %w_key.1, ...), custom_call_target="tpu_custom_call" | custom-call | tf_op jit(solution)/shard_map/pallas_call | solution.py:567
  104.0 5.2 %shard_map.141 = (f32[8,2,256,512]{3,2,1,0:T(8,128)}, bf16[32,2048]{1,0:T(8,128)(2,1)}) custom-call(bf16[8,2,256,512]{3,2,1,0:T(8,128)(2,1)} %get-tuple-element.6.x, bf16[32,2048]{1,0:T(8,128)(2,1)} %get-tuple-element.7.rows_in), custom_call_target="tpu_custom_call" | custom-call | tf_op jit(solution)/shard_map/pallas_call | solution.py:644
